TPU v7x, 32 devices: a whole 2x2x4 slice. The times are simulated.
32 devices in a mesh: dp: 16 (over z, y, core), feat: 2 (over x).
Axes of the slice: x: 2, y: 2, z: 4, core: 2. Of those that a mesh axis runs over, the one named last changes fastest.
Arguments:
- table: bfloat16 [2048, 3584], P('dp', 'feat'), may hold values from -64 to 64
- text: bfloat16 [2048, 3584], P('dp', 'feat'), may hold values from -64 to 64
- table_proj: bfloat16 [3584, 4096], P(None, 'feat'), may hold values from -1 to 1
- text_proj: bfloat16 [3584, 4096], P(None, 'feat'), may hold values from -1 to 1
Outputs:
- grad_table: float32 [2048, 3584], P('dp', 'feat')
- grad_text: float32 [2048, 3584], P('dp', 'feat')
- loss_mean: float32 [1], replicated
All inputs are finite; a program needn't handle non-finite values.
Results may differ from a plain program's by a relative error of at most 0.0044.
Values may be sent and summed in bfloat16 or wider, within the bound.
No kernel may reach another device: no remote copies, remote signals or barrier semaphores. Data moves between devices by JAX's collectives and lax.ppermute only.
A program may use at most 128 MiB of HBM per device.

v0:
```python
import jax
import jax.numpy as jnp
from jax import lax
from jax.experimental import pallas as pl
from jax.experimental.pallas import tpu as pltpu
from jax.sharding import Mesh
from jax.sharding import PartitionSpec as P

OFF_WEIGHT = 0.1
EPS = 1e-05
Z_CHIPS = 4
F32 = jnp.float32
BF16 = jnp.bfloat16


def dot(a, b, dims):
    return lax.dot_general(a, b, (dims, ((), ())), preferred_element_type=F32)


def shift(x, axis, step):
    size = lax.axis_size(axis)
    return lax.ppermute(x, axis, [(i, (i + step) % size) for i in range(size)])


def flip(x, axis, bit=1):
    size = lax.axis_size(axis)
    return lax.ppermute(x, axis, [(i, i ^ bit) for i in range(size)])


def cube_sum(x, *axes):
    for axis in axes:
        bit = 1
        while bit < lax.axis_size(axis):
            x = x + flip(x, axis, bit)
            bit *= 2
    return x


def own_block(x, index, count, axis):
    size = x.shape[axis] // count
    return lax.dynamic_slice_in_dim(x, index * size, size, axis)


def both_cores(x, axis=0):
    got = flip(x, "core")
    first = lax.axis_index("core") == 0
    return jnp.where(first, jnp.concatenate([x, got], axis), jnp.concatenate([got, x], axis))


def add_cores(x):
    core = lax.axis_index("core")
    return own_block(x, core, 2, 0) + flip(own_block(x, 1 - core, 2, 0), "core")


def cut_kernel(starts, *refs):
    sources, blocks, sems = refs[:2], refs[2:-1], refs[-1]
    count = len(blocks) // 2
    rows, cols = blocks[0].shape
    copies = []
    for i, block in enumerate(blocks):
        row = pl.multiple_of(starts[1 + i % count], 16)
        col = pl.multiple_of(starts[0], 128)
        source = sources[i // count].at[pl.ds(row, rows), pl.ds(col, cols)]
        copies.append(pltpu.make_async_copy(source, block, sems.at[i]))
    for copy in copies:
        copy.start()
    for copy in copies:
        copy.wait()


def weight_blocks(table_proj, text_proj):
    num_feat = lax.axis_size("feat")
    feat = lax.axis_index("feat")
    rows, cols = table_proj.shape[0] // num_feat, table_proj.shape[1] // 2
    firsts = [(feat - step) % num_feat * rows for step in range(num_feat)]
    starts = jnp.stack([lax.axis_index("core") * cols, *firsts]).astype(jnp.int32)
    count = 2 * num_feat
    blocks = pl.pallas_call(
        cut_kernel,
        out_shape=[jax.ShapeDtypeStruct((rows, cols), BF16)] * count,
        in_specs=[pl.BlockSpec(memory_space=pltpu.SMEM), pl.BlockSpec(memory_space=pl.ANY), pl.BlockSpec(memory_space=pl.ANY)],
        out_specs=[pl.BlockSpec(memory_space=pltpu.VMEM)] * count,
        scratch_shapes=[pltpu.SemaphoreType.DMA((count,))],
        compiler_params=pltpu.CompilerParams(vmem_limit_bytes=40 * 1024 * 1024),
    )(starts, table_proj, text_proj)
    return blocks[:num_feat], blocks[num_feat:]


def swap_feat(x):
    return [shift(x, "feat", step) for step in range(1, lax.axis_size("feat"))]


def moments(z_table, z_text):
    count = z_table.shape[0]
    mean_table, mean_text = jnp.mean(z_table, axis=0), jnp.mean(z_text, axis=0)
    centered_table, centered_text = z_table - mean_table, z_text - mean_text
    state = jnp.stack(
        [
            mean_table,
            mean_text,
            jnp.sum(centered_table * centered_table, axis=0),
            jnp.sum(centered_text * centered_text, axis=0),
            jnp.sum(centered_table * centered_text, axis=0),
        ]
    )
    for axis in ("z", "y"):
        bit = 1
        while bit < lax.axis_size(axis):
            other = flip(state, axis, bit)
            gap = state[:2] - other[:2]
            moved = (count / 2) * jnp.concatenate([gap * gap, gap[:1] * gap[1:]], 0)
            state = jnp.concatenate([(state[:2] + other[:2]) / 2, state[2:] + other[2:] + moved], 0)
            count *= 2
            bit *= 2
    return state[:2], state[2:] / count


def at_end(end, inner):
    z = lax.axis_index("z")
    return jnp.where((z == 0) | (z == Z_CHIPS - 1), end, inner)


def over_y(x):
    return [flip(x, "y", step) for step in range(1, lax.axis_size("y"))]


def gram_part(half, rows):
    return add_cores(dot(half, rows, ((1,), (1,))))


def add_feat(mine, others, axis):
    for other in others:
        mine = mine + other.astype(F32)
    return both_cores(mine.astype(BF16), axis)


def column_sums(d, normed):
    return jnp.stack([jnp.sum(d, axis=0), jnp.sum(d * normed, axis=0)])


def backward(d, normed, inverse, means):
    return (inverse * (d - means[0] - normed * means[1])).astype(BF16)


def swap_parts(sent):
    num_feat = lax.axis_size("feat")
    return [shift(part, "feat", num_feat - step) for step, part in enumerate(sent, 1)]


def body(table, text, table_proj, text_proj):
    pairs = table.shape[0] * 2 * lax.axis_size("z") * lax.axis_size("y")
    features = table_proj.shape[1] * lax.axis_size("feat")
    others_table, others_text = swap_feat(table), swap_feat(text)
    table_weights, text_weights = weight_blocks(table_proj, text_proj)
    z_table = dot(both_cores(table), table_weights[0], ((1,), (0,)))
    z_text = dot(both_cores(text), text_weights[0], ((1,), (0,)))
    z_table, z_text, others_table, others_text = lax.optimization_barrier((z_table, z_text, others_table, others_text))
    for other, weight in zip(others_table, table_weights[1:]):
        z_table = z_table + dot(both_cores(other), weight, ((1,), (0,)))
    for other, weight in zip(others_text, text_weights[1:]):
        z_text = z_text + dot(both_cores(other), weight, ((1,), (0,)))

    centers, spreads = moments(z_table, z_text)
    inverse_table, inverse_text = lax.rsqrt(spreads[0] + EPS), lax.rsqrt(spreads[1] + EPS)
    diag = inverse_table * inverse_text * spreads[2]
    diag_weight = (diag - 1.0).astype(BF16).astype(F32) - OFF_WEIGHT * diag
    normed_table = (z_table - centers[0]) * inverse_table
    normed_text = (z_text - centers[1]) * inverse_text
    half_table, half_text = normed_table.astype(BF16), normed_text.astype(BF16)

    half = jnp.stack([half_table, half_text])
    near, mid, y_own = lax.optimization_barrier((flip(half, "z"), lax.ppermute(half, "z", [(1, 2), (2, 1)]), over_y(half)))
    far_in, far_end, y_near = lax.optimization_barrier(
        (lax.ppermute(near, "z", [(1, 2), (2, 1)]), lax.ppermute(mid, "z", [(1, 0), (2, 3)]), over_y(near))
    )
    far = at_end(far_end, far_in)
    last_end, y_far = lax.optimization_barrier((lax.ppermute(far_in, "z", [(1, 0), (2, 3)]), over_y(far)))
    last = at_end(last_end, mid)
    cut = half.shape[1] // 2
    y_last = over_y(last[:, :cut])
    y_flip = [flip(block[:, cut:], "z") for block in y_far]

    early = [half, near, far, *y_own, *y_near, *y_far]
    early_table, early_text = [jnp.concatenate([block[i] for block in early], 0) for i in range(2)]
    gram_table = gram_part(half_table, early_table)
    others_table = swap_feat(gram_table.astype(BF16))
    gram_text = gram_part(half_text, early_text)
    others_text = swap_feat(gram_text.astype(BF16))
    y_last, y_flip, others_table, gram_text = lax.optimization_barrier((y_last, y_flip, others_table, gram_text))
    late = [last] + [block for pair in zip(y_last, y_flip) for block in pair]
    late_table, late_text = [jnp.concatenate([block[i] for block in late], 0) for i in range(2)]
    all_table, all_text = (early_table, late_table), (early_text, late_text)
    late_gram = jnp.concatenate([gram_part(half_table, late_table), gram_part(half_text, late_text)], 1)
    late_gram = add_feat(late_gram, swap_feat(late_gram.astype(BF16)), 0)
    gram_table = add_feat(gram_table, others_table, 0)
    gram_text = add_feat(gram_text, others_text, 0)
    grams = (gram_table, gram_text), jnp.split(late_gram, 2, 1)

    off_table, off_text = 0.0, 0.0
    for gram, rows_table, rows_text in zip(grams, all_table, all_text):
        off_table = off_table + dot(gram[1], rows_table, ((1,), (0,)))
        off_text = off_text + dot(gram[0], rows_text, ((1,), (0,)))
    d_table = (OFF_WEIGHT / pairs) * off_table + half_text.astype(F32) * diag_weight
    d_text = (OFF_WEIGHT / pairs) * off_text + half_table.astype(F32) * diag_weight
    sums = jnp.concatenate([column_sums(d_text, normed_text), column_sums(d_table, normed_table)], 0)
    means = cube_sum(sums, "z", "y") / pairs

    squares = means[3] - diag_weight * diag
    terms = (1.0 - diag) * (1.0 - diag) - OFF_WEIGHT * diag * diag + squares
    loss_total = cube_sum(jnp.sum(terms).reshape(1), "feat")

    back_text = backward(d_text, normed_text, inverse_text, means[:2])
    parts_text = [dot(back_text, weight, ((1,), (1,))) for weight in text_weights[1:]]
    d_table, parts_text = lax.optimization_barrier((d_table, parts_text))
    sent_text = [add_cores(part).astype(BF16) for part in parts_text]
    back_table = backward(d_table, normed_table, inverse_table, means[2:])
    parts_table = [dot(back_table, weight, ((1,), (1,))) for weight in table_weights[1:]]
    sent_text, parts_table, back_text, loss_total = lax.optimization_barrier((sent_text, parts_table, back_text, loss_total))
    sent_table = [add_cores(part).astype(BF16) for part in parts_table]
    sent = [jnp.stack(pair) for pair in zip(sent_text, sent_table)]
    own_text = dot(back_text, text_weights[0], ((1,), (1,)))
    own_table = dot(back_table, table_weights[0], ((1,), (1,)))
    own_text, own_table, sent = lax.optimization_barrier((own_text, own_table, sent))
    grads = swap_parts(sent)
    loss_total = cube_sum(loss_total, "core")
    grad_text = add_cores(own_text) + sum(part[0].astype(F32) for part in grads)
    grad_table = add_cores(own_table) + sum(part[1].astype(F32) for part in grads)
    return grad_table, grad_text, loss_total / features


def solution(mesh):
    devices = mesh.devices
    split = Mesh(
        devices.reshape(Z_CHIPS, devices.shape[0] // (2 * Z_CHIPS), 2, devices.shape[1]),
        ("z", "y", "core", "feat"),
    )
    rows = ("z", "y", "core")
    placed = (P(rows, "feat"), P(rows, "feat"), P(None, "feat"), P(None, "feat"))
    return jax.shard_map(
        body,
        mesh=split,
        in_specs=placed,
        out_specs=(P(rows, "feat"), P(rows, "feat"), P()),
        check_vma=False,
    )
```

profile of v0, /device:TPU:0, one launch (start us, length us, event | category | flops | bytes accessed | tf_op | source)
XLA Modules:
  0.0 215.6 jit_solution(3820881453166804329)
XLA Ops:
  1.2 2.9 %collective-permute-start.2 = (bf16[128,1792]{1,0:T(8,128)(2,1)}, bf16[128,1792]{1,0:T(8,128)(2,1)S(1)}, u32[]{:S(2)}, u32[]{:S(2)}) collective-permute-start(bf16[128,1792]{1,0:T(8,128)(2,1)} %param.4), channel_id=1, source_target_pairs={{0,1},{1,0},{2,3},{3,2},{4,5},{5,4},{6,7},{7,6},{8,9},{9,8},{10,11... | collective-permute-start | bytes 1376264 | tf_op jit(solution)/shard_map/ppermute | solution.py:22
  4.3 7.7 %shard_map.67 = (bf16[1792,1024]{1,0:T(8,128)(2,1)S(1)}, bf16[1792,1024]{1,0:T(8,128)(2,1)S(1)}, bf16[1792,1024]{1,0:T(8,128)(2,1)S(1)}, bf16[1792,1024]{1,0:T(8,128)(2,1)}) custom-call(s32[3]{0:T(128)S(1)} %pad_add_fusion.starts, bf16[3584,2048]{1,0:T(8,128)(2,1)} %refs_0_.1, bf16[3584,2048]{1,0:T(8,128)(2,1)} %refs_1_.1), custom_call_target="tpu_custom_call" | custom-call | tf_op jit(solution)/shard_map/pallas_call | solution.py:78
  16.0 8.9 %collective-permute-done.3 = bf16[128,1792]{1,0:T(8,128)(2,1)S(1)} collective-permute-done((bf16[128,1792]{1,0:T(8,128)(2,1)}, bf16[128,1792]{1,0:T(8,128)(2,1)S(1)}, u32[]{:S(2)}, u32[]{:S(2)}) %collective-permute-start.3) | collective-permute-done | bytes 458784 | tf_op jit(solution)/shard_map/ppermute | solution.py:22
  32.4 2.1 collective-permute-done.6
  34.5 2.9 %collective-permute-start.7 = (f32[5,1024]{1,0:T(8,128)S(1)}, f32[5,1024]{1,0:T(8,128)S(1)}, u32[]{:S(2)}, u32[]{:S(2)}) collective-permute-start(f32[5,1024]{1,0:T(8,128)S(1)} %pad_maximum_fusion.9), channel_id=1, source_target_pairs={{0,16},{8,24},{16,0},{24,8},{1,17},{9,25},{17,1},{25,9},{2,18},{10... | collective-permute-start | bytes 61448 | tf_op jit(solution)/shard_map/ppermute | solution.py:27
  37.4 2.0 collective-permute-done.7
  41.3 2.1 collective-permute-done.8
  49.1 3.5 %collective-permute-start.9 = (bf16[2,256,1024]{2,1,0:T(8,128)(2,1)S(1)}, bf16[2,256,1024]{2,1,0:T(8,128)(2,1)}, u32[]{:S(2)}, u32[]{:S(2)}) collective-permute-start(bf16[2,256,1024]{2,1,0:T(8,128)(2,1)S(1)} %pad_maximum_fusion), channel_id=1, source_target_pairs={{0,8},{8,0},{16,24},{24,16},{1,9},{9,1},{17,25},{25,17},{2,10},{10... | collective-permute-start | bytes 3145736 | tf_op jit(solution)/shard_map/ppermute | solution.py:27
  52.6 16.8 %collective-permute-done.11 = bf16[2,256,1024]{2,1,0:T(8,128)(2,1)} collective-permute-done((bf16[2,256,1024]{2,1,0:T(8,128)(2,1)S(1)}, bf16[2,256,1024]{2,1,0:T(8,128)(2,1)}, u32[]{:S(2)}, u32[]{:S(2)}) %collective-permute-start.11) | collective-permute-done | bytes 1048608 | tf_op jit(solution)/shard_map/ppermute | solution.py:27
  69.4 2.7 %collective-permute-done.9 = bf16[2,256,1024]{2,1,0:T(8,128)(2,1)} collective-permute-done((bf16[2,256,1024]{2,1,0:T(8,128)(2,1)S(1)}, bf16[2,256,1024]{2,1,0:T(8,128)(2,1)}, u32[]{:S(2)}, u32[]{:S(2)}) %collective-permute-start.9) | collective-permute-done | bytes 1048608 | tf_op jit(solution)/shard_map/ppermute | solution.py:27
  75.6 21.4 %collective-permute-done.13 = bf16[2,256,1024]{2,1,0:T(8,128)(2,1)} collective-permute-done((bf16[2,256,1024]{2,1,0:T(8,128)(2,1)}, bf16[2,256,1024]{2,1,0:T(8,128)(2,1)}, u32[]{:S(2)}, u32[]{:S(2)}) %collective-permute-start.13) | collective-permute-done | bytes 1048608 | tf_op jit(solution)/shard_map/ppermute | solution.py:174
  100.4 2.1 bitcast_dynamic-update-slice_fusion.3
  103.4 2.1 bitcast_dynamic-update-slice_fusion.2
  105.4 2.1 bitcast_dynamic-update-slice_fusion.1
  107.5 11.5 %collective-permute-done.16 = bf16[2,256,1024]{2,1,0:T(8,128)(2,1)S(1)} collective-permute-done((bf16[2,256,1024]{2,1,0:T(8,128)(2,1)S(1)}, bf16[2,256,1024]{2,1,0:T(8,128)(2,1)S(1)}, u32[]{:S(2)}, u32[]{:S(2)}) %collective-permute-start.16) | collective-permute-done | bytes 1048608 | tf_op jit(solution)/shard_map/ppermute | solution.py:27
  119.9 2.9 %fusion.92 = f32[256,1536]{1,0:T(8,128)S(1)} fusion(bf16[256,1024]{1,0:T(8,128)(2,1)S(1)} %get-tuple-element.73, bf16[1536,1024]{1,0:T(8,128)(2,1)} %get-tuple-element.88), kind=kOutput, calls=%fused_computation.184 | convolution fusion | flops 805306368 | bytes 5242880 | tf_op jit(solution)/shard_map/dot_general | solution.py:17
  125.5 3.8 %collective-permute-start.18 = (bf16[2,128,1024]{2,1,0:T(8,128)(2,1)S(1)}, bf16[2,128,1024]{2,1,0:T(8,128)(2,1)S(1)}, u32[]{:S(2)}, u32[]{:S(2)}) collective-permute-start(bf16[2,128,1024]{2,1,0:T(8,128)(2,1)S(1)} %slice.155), channel_id=1, source_target_pairs={{0,8},{8,0},{16,24},{24,16},{1,9},{9,1},{17,25},{25,17},{2,10},{10... | collective-permute-start | bytes 1572872 | tf_op jit(solution)/shard_map/ppermute | solution.py:27
  131.1 7.7 %collective-permute-done.17 = bf16[2,128,1024]{2,1,0:T(8,128)(2,1)S(1)} collective-permute-done((bf16[2,128,1024]{2,1,0:T(8,128)(2,1)S(1)}, bf16[2,128,1024]{2,1,0:T(8,128)(2,1)S(1)}, u32[]{:S(2)}, u32[]{:S(2)}) %collective-permute-start.17) | collective-permute-done | bytes 524320 | tf_op jit(solution)/shard_map/ppermute | solution.py:27
  138.8 2.3 %collective-permute-done.18 = bf16[2,128,1024]{2,1,0:T(8,128)(2,1)S(1)} collective-permute-done((bf16[2,128,1024]{2,1,0:T(8,128)(2,1)S(1)}, bf16[2,128,1024]{2,1,0:T(8,128)(2,1)S(1)}, u32[]{:S(2)}, u32[]{:S(2)}) %collective-permute-start.18) | collective-permute-done | bytes 524320 | tf_op jit(solution)/shard_map/ppermute | solution.py:27
  146.0 13.6 %collective-permute-done.26 = bf16[128,1024]{1,0:T(8,128)(2,1)S(1)} collective-permute-done((bf16[128,1024]{1,0:T(8,128)(2,1)S(1)}, bf16[128,1024]{1,0:T(8,128)(2,1)S(1)}, u32[]{:S(2)}, u32[]{:S(2)}) %collective-permute-start.26) | collective-permute-done | bytes 262176 | tf_op jit(solution)/shard_map/ppermute | solution.py:22
  168.1 2.0 collective-permute-done.29
  170.1 2.8 %collective-permute-start.30 = (f32[4,1024]{1,0:T(4,128)S(1)}, f32[4,1024]{1,0:T(4,128)S(1)}, u32[]{:S(2)}, u32[]{:S(2)}) collective-permute-start(f32[4,1024]{1,0:T(4,128)S(1)} %fusion.78), channel_id=1, source_target_pairs={{0,16},{8,24},{16,0},{24,8},{1,17},{9,25},{17,1},{25,9},{2,18},{10... | collective-permute-start | bytes 49160 | tf_op jit(solution)/shard_map/ppermute | solution.py:27
  176.4 2.2 %collective-permute-done.31 = f32[4,1024]{1,0:T(4,128)S(1)} collective-permute-done((f32[4,1024]{1,0:T(4,128)S(1)}, f32[4,1024]{1,0:T(4,128)S(1)}, u32[]{:S(2)}, u32[]{:S(2)}) %collective-permute-start.31) | collective-permute-done | bytes 16416 | tf_op jit(solution)/shard_map/ppermute | solution.py:27
  194.5 18.5 %collective-permute-done.36 = bf16[2,128,1792]{2,1,0:T(8,128)(2,1)S(1)} collective-permute-done((bf16[2,128,1792]{2,1,0:T(8,128)(2,1)S(1)}, bf16[2,128,1792]{2,1,0:T(8,128)(2,1)S(1)}, u32[]{:S(2)}, u32[]{:S(2)}) %collective-permute-start.36) | collective-permute-done | bytes 917536 | tf_op jit(solution)/shard_map/ppermute | solution.py:22
  (158 shorter events, 64.5 us)
Async XLA Ops:
  0.6 11.4 %collective-permute-start.1 = (bf16[128,1792]{1,0:T(8,128)(2,1)}, bf16[128,1792]{1,0:T(8,128)(2,1)S(1)}, u32[]{:S(2)}, u32[]{:S(2)}) collective-permute-start(bf16[128,1792]{1,0:T(8,128)(2,1)} %param.5), channel_id=1, source_target_pairs={{0,2},{2,0},{1,3},{3,1},{4,6},{6,4},{5,7},{7,5},{8,10},{10,8},{9,1... | collective-permute-start | bytes 1376264 | tf_op jit(solution)/shard_map/ppermute | solution.py:27
  1.1 12.6 %collective-permute-start = (bf16[128,1792]{1,0:T(8,128)(2,1)}, bf16[128,1792]{1,0:T(8,128)(2,1)S(1)}, u32[]{:S(2)}, u32[]{:S(2)}) collective-permute-start(bf16[128,1792]{1,0:T(8,128)(2,1)} %param.4), channel_id=1, source_target_pairs={{0,2},{2,0},{1,3},{3,1},{4,6},{6,4},{5,7},{7,5},{8,10},{10,8},{9,1... | collective-permute-start | bytes 1376264 | tf_op jit(solution)/shard_map/ppermute | solution.py:27
  1.2 14.8 %collective-permute-start.2 = (bf16[128,1792]{1,0:T(8,128)(2,1)}, bf16[128,1792]{1,0:T(8,128)(2,1)S(1)}, u32[]{:S(2)}, u32[]{:S(2)}) collective-permute-start(bf16[128,1792]{1,0:T(8,128)(2,1)} %param.4), channel_id=1, source_target_pairs={{0,1},{1,0},{2,3},{3,2},{4,5},{5,4},{6,7},{7,6},{8,9},{9,8},{10,11... | collective-permute-start | bytes 1376264 | tf_op jit(solution)/shard_map/ppermute | solution.py:22
  4.1 20.8 %collective-permute-start.3 = (bf16[128,1792]{1,0:T(8,128)(2,1)}, bf16[128,1792]{1,0:T(8,128)(2,1)S(1)}, u32[]{:S(2)}, u32[]{:S(2)}) collective-permute-start(bf16[128,1792]{1,0:T(8,128)(2,1)} %param.5), channel_id=1, source_target_pairs={{0,1},{1,0},{2,3},{3,2},{4,5},{5,4},{6,7},{7,6},{8,9},{9,8},{10,11... | collective-permute-start | bytes 1376264 | tf_op jit(solution)/shard_map/ppermute | solution.py:22
  34.5 4.9 %collective-permute-start.7 = (f32[5,1024]{1,0:T(8,128)S(1)}, f32[5,1024]{1,0:T(8,128)S(1)}, u32[]{:S(2)}, u32[]{:S(2)}) collective-permute-start(f32[5,1024]{1,0:T(8,128)S(1)} %pad_maximum_fusion.9), channel_id=1, source_target_pairs={{0,16},{8,24},{16,0},{24,8},{1,17},{9,25},{17,1},{25,9},{2,18},{10... | collective-permute-start | bytes 61448 | tf_op jit(solution)/shard_map/ppermute | solution.py:27
  45.7 6.9 %collective-permute-start.10 = (bf16[2,256,1024]{2,1,0:T(8,128)(2,1)S(1)}, bf16[2,256,1024]{2,1,0:T(8,128)(2,1)}, u32[]{:S(2)}, u32[]{:S(2)}) collective-permute-start(bf16[2,256,1024]{2,1,0:T(8,128)(2,1)S(1)} %pad_maximum_fusion), channel_id=1, source_target_pairs={{8,16},{16,8},{9,17},{17,9},{10,18},{18,10},{11,19},{19,11},{12,20... | collective-permute-start | bytes 3145736 | tf_op jit(solution)/shard_map/ppermute | solution.py:172
  47.3 22.1 %collective-permute-start.11 = (bf16[2,256,1024]{2,1,0:T(8,128)(2,1)S(1)}, bf16[2,256,1024]{2,1,0:T(8,128)(2,1)}, u32[]{:S(2)}, u32[]{:S(2)}) collective-permute-start(bf16[2,256,1024]{2,1,0:T(8,128)(2,1)S(1)} %pad_maximum_fusion), channel_id=1, source_target_pairs={{0,4},{4,0},{1,5},{5,1},{2,6},{6,2},{3,7},{7,3},{8,12},{12,8},{9,1... | collective-permute-start | bytes 3145736 | tf_op jit(solution)/shard_map/ppermute | solution.py:27
  49.1 23.0 %collective-permute-start.9 = (bf16[2,256,1024]{2,1,0:T(8,128)(2,1)S(1)}, bf16[2,256,1024]{2,1,0:T(8,128)(2,1)}, u32[]{:S(2)}, u32[]{:S(2)}) collective-permute-start(bf16[2,256,1024]{2,1,0:T(8,128)(2,1)S(1)} %pad_maximum_fusion), channel_id=1, source_target_pairs={{0,8},{8,0},{16,24},{24,16},{1,9},{9,1},{17,25},{25,17},{2,10},{10... | collective-permute-start | bytes 3145736 | tf_op jit(solution)/shard_map/ppermute | solution.py:27
  73.8 23.2 %collective-permute-start.13 = (bf16[2,256,1024]{2,1,0:T(8,128)(2,1)}, bf16[2,256,1024]{2,1,0:T(8,128)(2,1)}, u32[]{:S(2)}, u32[]{:S(2)}) collective-permute-start(bf16[2,256,1024]{2,1,0:T(8,128)(2,1)} %collective-permute-done.10), channel_id=1, source_target_pairs={{8,0},{16,24},{9,1},{17,25},{10,2},{18,26},{11,3},{19,27},{12,4},{... | collective-permute-start | bytes 3145736 | tf_op jit(solution)/shard_map/ppermute | solution.py:174
  75.1 21.9 %collective-permute-start.14 = (bf16[2,256,1024]{2,1,0:T(8,128)(2,1)}, bf16[2,256,1024]{2,1,0:T(8,128)(2,1)}, u32[]{:S(2)}, u32[]{:S(2)}) collective-permute-start(bf16[2,256,1024]{2,1,0:T(8,128)(2,1)} %collective-permute-done.9), channel_id=1, source_target_pairs={{0,4},{4,0},{1,5},{5,1},{2,6},{6,2},{3,7},{7,3},{8,12},{12,8},{9,1... | collective-permute-start | bytes 3145736 | tf_op jit(solution)/shard_map/ppermute | solution.py:27
  97.0 22.0 %collective-permute-start.15 = (bf16[2,256,1024]{2,1,0:T(8,128)(2,1)}, bf16[2,256,1024]{2,1,0:T(8,128)(2,1)S(1)}, u32[]{:S(2)}, u32[]{:S(2)}) collective-permute-start(bf16[2,256,1024]{2,1,0:T(8,128)(2,1)} %collective-permute-done.12), channel_id=1, source_target_pairs={{8,0},{16,24},{9,1},{17,25},{10,2},{18,26},{11,3},{19,27},{12,4},{... | collective-permute-start | bytes 3145736 | tf_op jit(solution)/shard_map/ppermute | solution.py:177
  99.8 19.2 %collective-permute-start.16 = (bf16[2,256,1024]{2,1,0:T(8,128)(2,1)S(1)}, bf16[2,256,1024]{2,1,0:T(8,128)(2,1)S(1)}, u32[]{:S(2)}, u32[]{:S(2)}) collective-permute-start(bf16[2,256,1024]{2,1,0:T(8,128)(2,1)S(1)} %broadcast_select_fusion.1), channel_id=1, source_target_pairs={{0,4},{4,0},{1,5},{5,1},{2,6},{6,2},{3,7},{7,3},{8,12},{12,8},{9,1... | collective-permute-start | bytes 3145736 | tf_op jit(solution)/shard_map/ppermute | solution.py:27
  123.9 5.4 %collective-permute-start.19 = (f32[128,1536]{1,0:T(8,128)S(1)}, f32[128,1536]{1,0:T(8,128)S(1)}, u32[]{:S(2)}, u32[]{:S(2)}) collective-permute-start(f32[128,1536]{1,0:T(8,128)S(1)} %constant_dynamic-slice_fusion.7), channel_id=1, source_target_pairs={{0,2},{2,0},{1,3},{3,1},{4,6},{6,4},{5,7},{7,5},{8,10},{10,8},{9,1... | collective-permute-start | bytes 2359304 | tf_op jit(solution)/shard_map/ppermute | solution.py:27
  124.1 6.9 %collective-permute-start.21 = (f32[128,1536]{1,0:T(8,128)S(1)}, f32[128,1536]{1,0:T(8,128)S(1)}, u32[]{:S(2)}, u32[]{:S(2)}) collective-permute-start(f32[128,1536]{1,0:T(8,128)S(1)} %constant_dynamic-slice_fusion.6), channel_id=1, source_target_pairs={{0,2},{2,0},{1,3},{3,1},{4,6},{6,4},{5,7},{7,5},{8,10},{10,8},{9,1... | collective-permute-start | bytes 2359304 | tf_op jit(solution)/shard_map/ppermute | solution.py:27
  124.9 13.9 %collective-permute-start.17 = (bf16[2,128,1024]{2,1,0:T(8,128)(2,1)S(1)}, bf16[2,128,1024]{2,1,0:T(8,128)(2,1)S(1)}, u32[]{:S(2)}, u32[]{:S(2)}) collective-permute-start(bf16[2,128,1024]{2,1,0:T(8,128)(2,1)S(1)} %slice.195), channel_id=1, source_target_pairs={{0,4},{4,0},{1,5},{5,1},{2,6},{6,2},{3,7},{7,3},{8,12},{12,8},{9,1... | collective-permute-start | bytes 1572872 | tf_op jit(solution)/shard_map/ppermute | solution.py:27
  125.5 15.6 %collective-permute-start.18 = (bf16[2,128,1024]{2,1,0:T(8,128)(2,1)S(1)}, bf16[2,128,1024]{2,1,0:T(8,128)(2,1)S(1)}, u32[]{:S(2)}, u32[]{:S(2)}) collective-permute-start(bf16[2,128,1024]{2,1,0:T(8,128)(2,1)S(1)} %slice.155), channel_id=1, source_target_pairs={{0,8},{8,0},{16,24},{24,16},{1,9},{9,1},{17,25},{25,17},{2,10},{10... | collective-permute-start | bytes 1572872 | tf_op jit(solution)/shard_map/ppermute | solution.py:27
  129.5 11.6 %collective-permute-start.20 = (bf16[128,1536]{1,0:T(8,128)(2,1)S(1)}, bf16[128,1536]{1,0:T(8,128)(2,1)S(1)}, u32[]{:S(2)}, u32[]{:S(2)}) collective-permute-start(bf16[128,1536]{1,0:T(8,128)(2,1)S(1)} %fusion.54), channel_id=1, source_target_pairs={{0,1},{1,0},{2,3},{3,2},{4,5},{5,4},{6,7},{7,6},{8,9},{9,8},{10,11... | collective-permute-start | bytes 1179656 | tf_op jit(solution)/shard_map/ppermute | solution.py:22
  142.9 16.9 %collective-permute-start.22 = (bf16[128,1536]{1,0:T(8,128)(2,1)S(1)}, bf16[128,1536]{1,0:T(8,128)(2,1)S(1)}, u32[]{:S(2)}, u32[]{:S(2)}) collective-permute-start(bf16[128,1536]{1,0:T(8,128)(2,1)S(1)} %get-tuple-element.70), channel_id=1, source_target_pairs={{0,1},{1,0},{2,3},{3,2},{4,5},{5,4},{6,7},{7,6},{8,9},{9,8},{10,11... | collective-permute-start | bytes 1179656 | tf_op jit(solution)/shard_map/ppermute | solution.py:22
  144.5 15.1 %collective-permute-start.26 = (bf16[128,1024]{1,0:T(8,128)(2,1)S(1)}, bf16[128,1024]{1,0:T(8,128)(2,1)S(1)}, u32[]{:S(2)}, u32[]{:S(2)}) collective-permute-start(bf16[128,1024]{1,0:T(8,128)(2,1)S(1)} %fusion.49), channel_id=1, source_target_pairs={{0,1},{1,0},{2,3},{3,2},{4,5},{5,4},{6,7},{7,6},{8,9},{9,8},{10,11... | collective-permute-start | bytes 786440 | tf_op jit(solution)/shard_map/ppermute | solution.py:22
  145.8 16.4 %collective-permute-start.28 = (bf16[128,1536]{1,0:T(8,128)(2,1)S(1)}, bf16[128,1536]{1,0:T(8,128)(2,1)S(1)}, u32[]{:S(2)}, u32[]{:S(2)}) collective-permute-start(bf16[128,1536]{1,0:T(8,128)(2,1)S(1)} %add_convert_fusion.2), channel_id=1, source_target_pairs={{0,2},{2,0},{1,3},{3,1},{4,6},{6,4},{5,7},{7,5},{8,10},{10,8},{9,1... | collective-permute-start | bytes 1179656 | tf_op jit(solution)/shard_map/ppermute | solution.py:27
  159.8 5.1 %collective-permute-start.23 = (bf16[128,1536]{1,0:T(8,128)(2,1)S(1)}, bf16[128,1536]{1,0:T(8,128)(2,1)S(1)}, u32[]{:S(2)}, u32[]{:S(2)}) collective-permute-start(bf16[128,1536]{1,0:T(8,128)(2,1)S(1)} %add_convert_fusion.3), channel_id=1, source_target_pairs={{0,2},{2,0},{1,3},{3,1},{4,6},{6,4},{5,7},{7,5},{8,10},{10,8},{9,1... | collective-permute-start | bytes 1179656 | tf_op jit(solution)/shard_map/ppermute | solution.py:27
  170.1 4.7 %collective-permute-start.30 = (f32[4,1024]{1,0:T(4,128)S(1)}, f32[4,1024]{1,0:T(4,128)S(1)}, u32[]{:S(2)}, u32[]{:S(2)}) collective-permute-start(f32[4,1024]{1,0:T(4,128)S(1)} %fusion.78), channel_id=1, source_target_pairs={{0,16},{8,24},{16,0},{24,8},{1,17},{9,25},{17,1},{25,9},{2,18},{10... | collective-permute-start | bytes 49160 | tf_op jit(solution)/shard_map/ppermute | solution.py:27
  180.2 6.0 %collective-permute-start.32 = (f32[128,1792]{1,0:T(8,128)S(1)}, f32[128,1792]{1,0:T(8,128)S(1)}, u32[]{:S(2)}, u32[]{:S(2)}) collective-permute-start(f32[128,1792]{1,0:T(8,128)S(1)} %constant_dynamic-slice_fusion.3), channel_id=1, source_target_pairs={{0,2},{2,0},{1,3},{3,1},{4,6},{6,4},{5,7},{7,5},{8,10},{10,8},{9,1... | collective-permute-start | bytes 2752520 | tf_op jit(solution)/shard_map/ppermute | solution.py:27
  190.6 22.3 %collective-permute-start.36 = (bf16[2,128,1792]{2,1,0:T(8,128)(2,1)S(1)}, bf16[2,128,1792]{2,1,0:T(8,128)(2,1)S(1)}, u32[]{:S(2)}, u32[]{:S(2)}) collective-permute-start(bf16[2,128,1792]{2,1,0:T(8,128)(2,1)S(1)} %pad_maximum_fusion.3), channel_id=1, source_target_pairs={{0,1},{1,0},{2,3},{3,2},{4,5},{5,4},{6,7},{7,6},{8,9},{9,8},{10,11... | collective-permute-start | bytes 2752520 | tf_op jit(solution)/shard_map/ppermute | solution.py:22
  (27 other events, 128.3 us)
where the time goes:
time: 216 us
  waiting for transfers between devices  119 us (55%)
  starting transfers between devices  45.2 us (21%)
  matrix products  17.5 us (8%)
  local copies, waits for them, and re-layouts  13.2 us (6%)
  other arithmetic  8.35 us (4%)
  Pallas kernels  7.73 us (4%)
  between operations  4.59 us (2%)
    ppermute x29, waiting for transfers between devices, flip(): return lax.ppermute(x, axis, [(i, i ^ bit) for i in range(size)])  56.7 us
    ppermute x6, waiting for transfers between devices, shift(): return lax.ppermute(x, axis, [(i, (i + step) % size) for i in range(size)])  41 us
    ppermute x29, starting transfers between devices, flip(): return lax.ppermute(x, axis, [(i, i ^ bit) for i in range(size)])  30.7 us
    ppermute x1, waiting for transfers between devices, body(): lax.ppermute(mid, 'z', [(1, 0), (2, 3)])  21.4 us
    dot_general x16, matrix products, dot(): return lax.dot_general(a, b, (dims, ((), ())), preferred_element_type=F32)  17.5 us
    unnamed x28, local copies, waits for them, and re-layouts  11.5 us
    ppermute x6, starting transfers between devices, shift(): return lax.ppermute(x, axis, [(i, (i + step) % size) for i in range(size)])  8.43 us
    pallas_call x1, Pallas kernels, weight_blocks(): pl.pallas_call(cut_kernel, out_shape=[jax.ShapeDtypeStruct((rows, cols),...  7.73 us
  transfers between devices with their start and end apart: 39, of which 19 were waited for; matrix products, arithmetic and copies ran while one was open for 9% of the time, Pallas kernels for 4%

commit v1 on v0

--- a/solution.py
+++ b/solution.py
@@ -185,15 +185,17 @@
     gram_table = gram_part(half_table, early_table)
     others_table = swap_feat(gram_table.astype(BF16))
     gram_text = gram_part(half_text, early_text)
-    others_text = swap_feat(gram_text.astype(BF16))
-    y_last, y_flip, others_table, gram_text = lax.optimization_barrier((y_last, y_flip, others_table, gram_text))
+    gram_text = jnp.split(gram_text, 2, 1)
+    others_text = [swap_feat(part.astype(BF16)) for part in gram_text]
+    y_last, y_flip, others_table, others_text[0] = lax.optimization_barrier((y_last, y_flip, others_table, others_text[0]))
     late = [last] + [block for pair in zip(y_last, y_flip) for block in pair]
     late_table, late_text = [jnp.concatenate([block[i] for block in late], 0) for i in range(2)]
     all_table, all_text = (early_table, late_table), (early_text, late_text)
     late_gram = jnp.concatenate([gram_part(half_table, late_table), gram_part(half_text, late_text)], 1)
     late_gram = add_feat(late_gram, swap_feat(late_gram.astype(BF16)), 0)
     gram_table = add_feat(gram_table, others_table, 0)
-    gram_text = add_feat(gram_text, others_text, 0)
+    others_text = [jnp.concatenate(parts, 1) for parts in zip(*others_text)]
+    gram_text = add_feat(jnp.concatenate(gram_text, 1), others_text, 0)
     grams = (gram_table, gram_text), jnp.split(late_gram, 2, 1)
 
     off_table, off_text = 0.0, 0.0

time: 216 us -> 212 us (0.981)
  starting transfers between devices: 45.2 us -> 42.2 us
    ppermute x29, starting transfers between devices: 30.7 us -> 27.2 us  [flip(): return lax.ppermute(x, axis, [(i, i ^ bit) for i in range(size)])]
    ppermute x29, waiting for transfers between devices: 56.7 us -> 59.3 us  [flip(): return lax.ppermute(x, axis, [(i, i ^ bit) for i in range(size)])]
    ppermute x6 -> x7, waiting for transfers between devices: 41 us -> 39.9 us  [shift(): return lax.ppermute(x, axis, [(i, (i + step) % size) for i in range(size)])]
    ppermute x6 -> x7, starting transfers between devices: 8.43 us -> 8.97 us  [shift(): return lax.ppermute(x, axis, [(i, (i + step) % size) for i in range(size)])]
  transfers between devices with their start and end apart: 39 -> 40, of which waited for: 19 -> 20; matrix products, arithmetic and copies ran while one was open for 9% -> 10% of each run, Pallas kernels for 4% -> 4%
where the time goes in v1:
time: 212 us
  waiting for transfers between devices  121 us (57%)
  starting transfers between devices  42.2 us (20%)
  matrix products  15.7 us (7%)
  local copies, waits for them, and re-layouts  12.5 us (6%)
  other arithmetic  8.43 us (4%)
  Pallas kernels  7.73 us (4%)
  between operations  4.75 us (2%)
    ppermute x29, waiting for transfers between devices, flip(): return lax.ppermute(x, axis, [(i, i ^ bit) for i in range(size)])  59.3 us
    ppermute x7, waiting for transfers between devices, shift(): return lax.ppermute(x, axis, [(i, (i + step) % size) for i in range(size)])  39.9 us
    ppermute x29, starting transfers between devices, flip(): return lax.ppermute(x, axis, [(i, i ^ bit) for i in range(size)])  27.2 us
    ppermute x1, waiting for transfers between devices, body(): lax.ppermute(mid, 'z', [(1, 0), (2, 3)])  21.4 us
    dot_general x16, matrix products, dot(): return lax.dot_general(a, b, (dims, ((), ())), preferred_element_type=F32)  15.7 us
    unnamed x28, local copies, waits for them, and re-layouts  10.8 us
    ppermute x7, starting transfers between devices, shift(): return lax.ppermute(x, axis, [(i, (i + step) % size) for i in range(size)])  8.97 us
    pallas_call x1, Pallas kernels, weight_blocks(): pl.pallas_call(cut_kernel, out_shape=[jax.ShapeDtypeStruct((rows, cols),...  7.73 us
  transfers between devices with their start and end apart: 40, of which 20 were waited for; matrix products, arithmetic and copies ran while one was open for 10% of the time, Pallas kernels for 4%

profile of v1, /device:TPU:0, one launch (start us, length us, event | category | flops | bytes accessed | tf_op | source)
XLA Modules:
  0.0 211.8 jit_solution(14695238380445002282)
XLA Ops:
  1.2 2.9 %collective-permute-start.2 = (bf16[128,1792]{1,0:T(8,128)(2,1)}, bf16[128,1792]{1,0:T(8,128)(2,1)S(1)}, u32[]{:S(2)}, u32[]{:S(2)}) collective-permute-start(bf16[128,1792]{1,0:T(8,128)(2,1)} %param.4), channel_id=1, source_target_pairs={{0,1},{1,0},{2,3},{3,2},{4,5},{5,4},{6,7},{7,6},{8,9},{9,8},{10,11... | collective-permute-start | bytes 1376264 | tf_op jit(solution)/shard_map/ppermute | solution.py:22
  4.3 7.7 %shard_map.67 = (bf16[1792,1024]{1,0:T(8,128)(2,1)S(1)}, bf16[1792,1024]{1,0:T(8,128)(2,1)S(1)}, bf16[1792,1024]{1,0:T(8,128)(2,1)S(1)}, bf16[1792,1024]{1,0:T(8,128)(2,1)}) custom-call(s32[3]{0:T(128)S(1)} %pad_add_fusion.starts, bf16[3584,2048]{1,0:T(8,128)(2,1)} %refs_0_.1, bf16[3584,2048]{1,0:T(8,128)(2,1)} %refs_1_.1), custom_call_target="tpu_custom_call" | custom-call | tf_op jit(solution)/shard_map/pallas_call | solution.py:78
  16.0 8.9 %collective-permute-done.3 = bf16[128,1792]{1,0:T(8,128)(2,1)S(1)} collective-permute-done((bf16[128,1792]{1,0:T(8,128)(2,1)}, bf16[128,1792]{1,0:T(8,128)(2,1)S(1)}, u32[]{:S(2)}, u32[]{:S(2)}) %collective-permute-start.3) | collective-permute-done | bytes 458784 | tf_op jit(solution)/shard_map/ppermute | solution.py:22
  32.4 2.1 collective-permute-done.6
  34.5 2.9 %collective-permute-start.7 = (f32[5,1024]{1,0:T(8,128)S(1)}, f32[5,1024]{1,0:T(8,128)S(1)}, u32[]{:S(2)}, u32[]{:S(2)}) collective-permute-start(f32[5,1024]{1,0:T(8,128)S(1)} %pad_maximum_fusion.9), channel_id=1, source_target_pairs={{0,16},{8,24},{16,0},{24,8},{1,17},{9,25},{17,1},{25,9},{2,18},{10... | collective-permute-start | bytes 61448 | tf_op jit(solution)/shard_map/ppermute | solution.py:27
  37.4 2.0 collective-permute-done.7
  41.3 2.1 %collective-permute-done.8 = f32[5,1024]{1,0:T(8,128)S(1)} collective-permute-done((f32[5,1024]{1,0:T(8,128)S(1)}, f32[5,1024]{1,0:T(8,128)S(1)}, u32[]{:S(2)}, u32[]{:S(2)}) %collective-permute-start.8) | collective-permute-done | bytes 20512 | tf_op jit(solution)/shard_map/ppermute | solution.py:27
  49.1 3.5 %collective-permute-start.9 = (bf16[2,256,1024]{2,1,0:T(8,128)(2,1)S(1)}, bf16[2,256,1024]{2,1,0:T(8,128)(2,1)}, u32[]{:S(2)}, u32[]{:S(2)}) collective-permute-start(bf16[2,256,1024]{2,1,0:T(8,128)(2,1)S(1)} %pad_maximum_fusion), channel_id=1, source_target_pairs={{0,8},{8,0},{16,24},{24,16},{1,9},{9,1},{17,25},{25,17},{2,10},{10... | collective-permute-start | bytes 3145736 | tf_op jit(solution)/shard_map/ppermute | solution.py:27
  52.6 16.8 %collective-permute-done.11 = bf16[2,256,1024]{2,1,0:T(8,128)(2,1)} collective-permute-done((bf16[2,256,1024]{2,1,0:T(8,128)(2,1)S(1)}, bf16[2,256,1024]{2,1,0:T(8,128)(2,1)}, u32[]{:S(2)}, u32[]{:S(2)}) %collective-permute-start.11) | collective-permute-done | bytes 1048608 | tf_op jit(solution)/shard_map/ppermute | solution.py:27
  69.4 2.8 %collective-permute-done.9 = bf16[2,256,1024]{2,1,0:T(8,128)(2,1)} collective-permute-done((bf16[2,256,1024]{2,1,0:T(8,128)(2,1)S(1)}, bf16[2,256,1024]{2,1,0:T(8,128)(2,1)}, u32[]{:S(2)}, u32[]{:S(2)}) %collective-permute-start.9) | collective-permute-done | bytes 1048608 | tf_op jit(solution)/shard_map/ppermute | solution.py:27
  75.7 21.4 %collective-permute-done.13 = bf16[2,256,1024]{2,1,0:T(8,128)(2,1)} collective-permute-done((bf16[2,256,1024]{2,1,0:T(8,128)(2,1)}, bf16[2,256,1024]{2,1,0:T(8,128)(2,1)}, u32[]{:S(2)}, u32[]{:S(2)}) %collective-permute-start.13) | collective-permute-done | bytes 1048608 | tf_op jit(solution)/shard_map/ppermute | solution.py:174
  100.4 2.1 bitcast_dynamic-update-slice_fusion.7
  103.4 2.1 bitcast_dynamic-update-slice_fusion.6
  105.5 2.1 bitcast_dynamic-update-slice_fusion.5
  107.5 11.5 %collective-permute-done.16 = bf16[2,256,1024]{2,1,0:T(8,128)(2,1)S(1)} collective-permute-done((bf16[2,256,1024]{2,1,0:T(8,128)(2,1)S(1)}, bf16[2,256,1024]{2,1,0:T(8,128)(2,1)S(1)}, u32[]{:S(2)}, u32[]{:S(2)}) %collective-permute-start.16) | collective-permute-done | bytes 1048608 | tf_op jit(solution)/shard_map/ppermute | solution.py:27
  123.8 3.8 %collective-permute-start.19 = (bf16[2,128,1024]{2,1,0:T(8,128)(2,1)S(1)}, bf16[2,128,1024]{2,1,0:T(8,128)(2,1)S(1)}, u32[]{:S(2)}, u32[]{:S(2)}) collective-permute-start(bf16[2,128,1024]{2,1,0:T(8,128)(2,1)S(1)} %slice.161), channel_id=1, source_target_pairs={{0,8},{8,0},{16,24},{24,16},{1,9},{9,1},{17,25},{25,17},{2,10},{10... | collective-permute-start | bytes 1572872 | tf_op jit(solution)/shard_map/ppermute | solution.py:27
  130.1 7.5 %collective-permute-done.18 = bf16[2,128,1024]{2,1,0:T(8,128)(2,1)S(1)} collective-permute-done((bf16[2,128,1024]{2,1,0:T(8,128)(2,1)S(1)}, bf16[2,128,1024]{2,1,0:T(8,128)(2,1)S(1)}, u32[]{:S(2)}, u32[]{:S(2)}) %collective-permute-start.18) | collective-permute-done | bytes 524320 | tf_op jit(solution)/shard_map/ppermute | solution.py:27
  137.6 2.3 %collective-permute-done.19 = bf16[2,128,1024]{2,1,0:T(8,128)(2,1)S(1)} collective-permute-done((bf16[2,128,1024]{2,1,0:T(8,128)(2,1)S(1)}, bf16[2,128,1024]{2,1,0:T(8,128)(2,1)S(1)}, u32[]{:S(2)}, u32[]{:S(2)}) %collective-permute-start.19) | collective-permute-done | bytes 524320 | tf_op jit(solution)/shard_map/ppermute | solution.py:27
  139.9 3.0 %collective-permute-done.22 = bf16[128,768]{1,0:T(8,128)(2,1)S(1)} collective-permute-done((bf16[128,768]{1,0:T(8,128)(2,1)S(1)}, bf16[128,768]{1,0:T(8,128)(2,1)S(1)}, u32[]{:S(2)}, u32[]{:S(2)}) %collective-permute-start.22) | collective-permute-done | bytes 196640 | tf_op jit(solution)/shard_map/ppermute | solution.py:22
  147.8 9.4 %collective-permute-done.27 = bf16[128,1024]{1,0:T(8,128)(2,1)S(1)} collective-permute-done((bf16[128,1024]{1,0:T(8,128)(2,1)S(1)}, bf16[128,1024]{1,0:T(8,128)(2,1)S(1)}, u32[]{:S(2)}, u32[]{:S(2)}) %collective-permute-start.27) | collective-permute-done | bytes 262176 | tf_op jit(solution)/shard_map/ppermute | solution.py:22
  162.8 3.5 %collective-permute-done.30 = f32[4,1024]{1,0:T(4,128)S(1)} collective-permute-done((f32[4,1024]{1,0:T(4,128)S(1)}, f32[4,1024]{1,0:T(4,128)S(1)}, u32[]{:S(2)}, u32[]{:S(2)}) %collective-permute-start.30) | collective-permute-done | bytes 16416 | tf_op jit(solution)/shard_map/ppermute | solution.py:27
  167.6 3.4 %collective-permute-done.31 = f32[4,1024]{1,0:T(4,128)S(1)} collective-permute-done((f32[4,1024]{1,0:T(4,128)S(1)}, f32[4,1024]{1,0:T(4,128)S(1)}, u32[]{:S(2)}, u32[]{:S(2)}) %collective-permute-start.31) | collective-permute-done | bytes 16416 | tf_op jit(solution)/shard_map/ppermute | solution.py:27
  172.6 2.2 %collective-permute-done.32 = f32[4,1024]{1,0:T(4,128)S(1)} collective-permute-done((f32[4,1024]{1,0:T(4,128)S(1)}, f32[4,1024]{1,0:T(4,128)S(1)}, u32[]{:S(2)}, u32[]{:S(2)}) %collective-permute-start.32) | collective-permute-done | bytes 16416 | tf_op jit(solution)/shard_map/ppermute | solution.py:27
  190.5 18.6 %collective-permute-done.37 = bf16[2,128,1792]{2,1,0:T(8,128)(2,1)S(1)} collective-permute-done((bf16[2,128,1792]{2,1,0:T(8,128)(2,1)S(1)}, bf16[2,128,1792]{2,1,0:T(8,128)(2,1)S(1)}, u32[]{:S(2)}, u32[]{:S(2)}) %collective-permute-start.37) | collective-permute-done | bytes 917536 | tf_op jit(solution)/shard_map/ppermute | solution.py:22
  (161 shorter events, 62.5 us)
Async XLA Ops:
  0.6 11.4 %collective-permute-start.1 = (bf16[128,1792]{1,0:T(8,128)(2,1)}, bf16[128,1792]{1,0:T(8,128)(2,1)S(1)}, u32[]{:S(2)}, u32[]{:S(2)}) collective-permute-start(bf16[128,1792]{1,0:T(8,128)(2,1)} %param.5), channel_id=1, source_target_pairs={{0,2},{2,0},{1,3},{3,1},{4,6},{6,4},{5,7},{7,5},{8,10},{10,8},{9,1... | collective-permute-start | bytes 1376264 | tf_op jit(solution)/shard_map/ppermute | solution.py:27
  1.1 12.6 %collective-permute-start = (bf16[128,1792]{1,0:T(8,128)(2,1)}, bf16[128,1792]{1,0:T(8,128)(2,1)S(1)}, u32[]{:S(2)}, u32[]{:S(2)}) collective-permute-start(bf16[128,1792]{1,0:T(8,128)(2,1)} %param.4), channel_id=1, source_target_pairs={{0,2},{2,0},{1,3},{3,1},{4,6},{6,4},{5,7},{7,5},{8,10},{10,8},{9,1... | collective-permute-start | bytes 1376264 | tf_op jit(solution)/shard_map/ppermute | solution.py:27
  1.2 14.8 %collective-permute-start.2 = (bf16[128,1792]{1,0:T(8,128)(2,1)}, bf16[128,1792]{1,0:T(8,128)(2,1)S(1)}, u32[]{:S(2)}, u32[]{:S(2)}) collective-permute-start(bf16[128,1792]{1,0:T(8,128)(2,1)} %param.4), channel_id=1, source_target_pairs={{0,1},{1,0},{2,3},{3,2},{4,5},{5,4},{6,7},{7,6},{8,9},{9,8},{10,11... | collective-permute-start | bytes 1376264 | tf_op jit(solution)/shard_map/ppermute | solution.py:22
  4.1 20.8 %collective-permute-start.3 = (bf16[128,1792]{1,0:T(8,128)(2,1)}, bf16[128,1792]{1,0:T(8,128)(2,1)S(1)}, u32[]{:S(2)}, u32[]{:S(2)}) collective-permute-start(bf16[128,1792]{1,0:T(8,128)(2,1)} %param.5), channel_id=1, source_target_pairs={{0,1},{1,0},{2,3},{3,2},{4,5},{5,4},{6,7},{7,6},{8,9},{9,8},{10,11... | collective-permute-start | bytes 1376264 | tf_op jit(solution)/shard_map/ppermute | solution.py:22
  34.5 4.9 %collective-permute-start.7 = (f32[5,1024]{1,0:T(8,128)S(1)}, f32[5,1024]{1,0:T(8,128)S(1)}, u32[]{:S(2)}, u32[]{:S(2)}) collective-permute-start(f32[5,1024]{1,0:T(8,128)S(1)} %pad_maximum_fusion.9), channel_id=1, source_target_pairs={{0,16},{8,24},{16,0},{24,8},{1,17},{9,25},{17,1},{25,9},{2,18},{10... | collective-permute-start | bytes 61448 | tf_op jit(solution)/shard_map/ppermute | solution.py:27
  45.7 6.9 %collective-permute-start.10 = (bf16[2,256,1024]{2,1,0:T(8,128)(2,1)S(1)}, bf16[2,256,1024]{2,1,0:T(8,128)(2,1)}, u32[]{:S(2)}, u32[]{:S(2)}) collective-permute-start(bf16[2,256,1024]{2,1,0:T(8,128)(2,1)S(1)} %pad_maximum_fusion), channel_id=1, source_target_pairs={{8,16},{16,8},{9,17},{17,9},{10,18},{18,10},{11,19},{19,11},{12,20... | collective-permute-start | bytes 3145736 | tf_op jit(solution)/shard_map/ppermute | solution.py:172
  47.3 22.1 %collective-permute-start.11 = (bf16[2,256,1024]{2,1,0:T(8,128)(2,1)S(1)}, bf16[2,256,1024]{2,1,0:T(8,128)(2,1)}, u32[]{:S(2)}, u32[]{:S(2)}) collective-permute-start(bf16[2,256,1024]{2,1,0:T(8,128)(2,1)S(1)} %pad_maximum_fusion), channel_id=1, source_target_pairs={{0,4},{4,0},{1,5},{5,1},{2,6},{6,2},{3,7},{7,3},{8,12},{12,8},{9,1... | collective-permute-start | bytes 3145736 | tf_op jit(solution)/shard_map/ppermute | solution.py:27
  49.1 23.0 %collective-permute-start.9 = (bf16[2,256,1024]{2,1,0:T(8,128)(2,1)S(1)}, bf16[2,256,1024]{2,1,0:T(8,128)(2,1)}, u32[]{:S(2)}, u32[]{:S(2)}) collective-permute-start(bf16[2,256,1024]{2,1,0:T(8,128)(2,1)S(1)} %pad_maximum_fusion), channel_id=1, source_target_pairs={{0,8},{8,0},{16,24},{24,16},{1,9},{9,1},{17,25},{25,17},{2,10},{10... | collective-permute-start | bytes 3145736 | tf_op jit(solution)/shard_map/ppermute | solution.py:27
  73.8 23.2 %collective-permute-start.13 = (bf16[2,256,1024]{2,1,0:T(8,128)(2,1)}, bf16[2,256,1024]{2,1,0:T(8,128)(2,1)}, u32[]{:S(2)}, u32[]{:S(2)}) collective-permute-start(bf16[2,256,1024]{2,1,0:T(8,128)(2,1)} %collective-permute-done.10), channel_id=1, source_target_pairs={{8,0},{16,24},{9,1},{17,25},{10,2},{18,26},{11,3},{19,27},{12,4},{... | collective-permute-start | bytes 3145736 | tf_op jit(solution)/shard_map/ppermute | solution.py:174
  75.1 22.0 %collective-permute-start.14 = (bf16[2,256,1024]{2,1,0:T(8,128)(2,1)}, bf16[2,256,1024]{2,1,0:T(8,128)(2,1)}, u32[]{:S(2)}, u32[]{:S(2)}) collective-permute-start(bf16[2,256,1024]{2,1,0:T(8,128)(2,1)} %collective-permute-done.9), channel_id=1, source_target_pairs={{0,4},{4,0},{1,5},{5,1},{2,6},{6,2},{3,7},{7,3},{8,12},{12,8},{9,1... | collective-permute-start | bytes 3145736 | tf_op jit(solution)/shard_map/ppermute | solution.py:27
  97.0 22.0 %collective-permute-start.15 = (bf16[2,256,1024]{2,1,0:T(8,128)(2,1)}, bf16[2,256,1024]{2,1,0:T(8,128)(2,1)S(1)}, u32[]{:S(2)}, u32[]{:S(2)}) collective-permute-start(bf16[2,256,1024]{2,1,0:T(8,128)(2,1)} %collective-permute-done.12), channel_id=1, source_target_pairs={{8,0},{16,24},{9,1},{17,25},{10,2},{18,26},{11,3},{19,27},{12,4},{... | collective-permute-start | bytes 3145736 | tf_op jit(solution)/shard_map/ppermute | solution.py:177
  99.8 19.2 %collective-permute-start.16 = (bf16[2,256,1024]{2,1,0:T(8,128)(2,1)S(1)}, bf16[2,256,1024]{2,1,0:T(8,128)(2,1)S(1)}, u32[]{:S(2)}, u32[]{:S(2)}) collective-permute-start(bf16[2,256,1024]{2,1,0:T(8,128)(2,1)S(1)} %broadcast_select_fusion.1), channel_id=1, source_target_pairs={{0,4},{4,0},{1,5},{5,1},{2,6},{6,2},{3,7},{7,3},{8,12},{12,8},{9,1... | collective-permute-start | bytes 3145736 | tf_op jit(solution)/shard_map/ppermute | solution.py:27
  121.1 6.5 %collective-permute-start.20 = (f32[128,1536]{1,0:T(8,128)S(1)}, f32[128,1536]{1,0:T(8,128)S(1)}, u32[]{:S(2)}, u32[]{:S(2)}) collective-permute-start(f32[128,1536]{1,0:T(8,128)S(1)} %constant_dynamic-slice_fusion.6), channel_id=1, source_target_pairs={{0,2},{2,0},{1,3},{3,1},{4,6},{6,4},{5,7},{7,5},{8,10},{10,8},{9,1... | collective-permute-start | bytes 2359304 | tf_op jit(solution)/shard_map/ppermute | solution.py:27
  123.0 6.3 %collective-permute-start.17 = (f32[128,1536]{1,0:T(8,128)S(1)}, f32[128,1536]{1,0:T(8,128)S(1)}, u32[]{:S(2)}, u32[]{:S(2)}) collective-permute-start(f32[128,1536]{1,0:T(8,128)S(1)} %constant_dynamic-slice_fusion.7), channel_id=1, source_target_pairs={{0,2},{2,0},{1,3},{3,1},{4,6},{6,4},{5,7},{7,5},{8,10},{10,8},{9,1... | collective-permute-start | bytes 2359304 | tf_op jit(solution)/shard_map/ppermute | solution.py:27
  123.2 14.4 %collective-permute-start.18 = (bf16[2,128,1024]{2,1,0:T(8,128)(2,1)S(1)}, bf16[2,128,1024]{2,1,0:T(8,128)(2,1)S(1)}, u32[]{:S(2)}, u32[]{:S(2)}) collective-permute-start(bf16[2,128,1024]{2,1,0:T(8,128)(2,1)S(1)} %slice.197), channel_id=1, source_target_pairs={{0,4},{4,0},{1,5},{5,1},{2,6},{6,2},{3,7},{7,3},{8,12},{12,8},{9,1... | collective-permute-start | bytes 1572872 | tf_op jit(solution)/shard_map/ppermute | solution.py:27
  123.8 16.1 %collective-permute-start.19 = (bf16[2,128,1024]{2,1,0:T(8,128)(2,1)S(1)}, bf16[2,128,1024]{2,1,0:T(8,128)(2,1)S(1)}, u32[]{:S(2)}, u32[]{:S(2)}) collective-permute-start(bf16[2,128,1024]{2,1,0:T(8,128)(2,1)S(1)} %slice.161), channel_id=1, source_target_pairs={{0,8},{8,0},{16,24},{24,16},{1,9},{9,1},{17,25},{25,17},{2,10},{10... | collective-permute-start | bytes 1572872 | tf_op jit(solution)/shard_map/ppermute | solution.py:27
  127.7 15.2 %collective-permute-start.21 = (bf16[128,1536]{1,0:T(8,128)(2,1)S(1)}, bf16[128,1536]{1,0:T(8,128)(2,1)S(1)}, u32[]{:S(2)}, u32[]{:S(2)}) collective-permute-start(bf16[128,1536]{1,0:T(8,128)(2,1)S(1)} %fusion.55), channel_id=1, source_target_pairs={{0,1},{1,0},{2,3},{3,2},{4,5},{5,4},{6,7},{7,6},{8,9},{9,8},{10,11... | collective-permute-start | bytes 1179656 | tf_op jit(solution)/shard_map/ppermute | solution.py:22
  129.5 13.5 %collective-permute-start.22 = (bf16[128,768]{1,0:T(8,128)(2,1)S(1)}, bf16[128,768]{1,0:T(8,128)(2,1)S(1)}, u32[]{:S(2)}, u32[]{:S(2)}) collective-permute-start(bf16[128,768]{1,0:T(8,128)(2,1)S(1)} %get-tuple-element.103), channel_id=1, source_target_pairs={{0,1},{1,0},{2,3},{3,2},{4,5},{5,4},{6,7},{7,6},{8,9},{9,8},{10,11... | collective-permute-start | bytes 589832 | tf_op jit(solution)/shard_map/ppermute | solution.py:22
  144.7 12.6 %collective-permute-start.23 = (bf16[128,768]{1,0:T(8,128)(2,1)S(1)}, bf16[128,768]{1,0:T(8,128)(2,1)S(1)}, u32[]{:S(2)}, u32[]{:S(2)}) collective-permute-start(bf16[128,768]{1,0:T(8,128)(2,1)S(1)} %get-tuple-element.102), channel_id=1, source_target_pairs={{0,1},{1,0},{2,3},{3,2},{4,5},{5,4},{6,7},{7,6},{8,9},{9,8},{10,11... | collective-permute-start | bytes 589832 | tf_op jit(solution)/shard_map/ppermute | solution.py:22
  146.4 10.8 %collective-permute-start.27 = (bf16[128,1024]{1,0:T(8,128)(2,1)S(1)}, bf16[128,1024]{1,0:T(8,128)(2,1)S(1)}, u32[]{:S(2)}, u32[]{:S(2)}) collective-permute-start(bf16[128,1024]{1,0:T(8,128)(2,1)S(1)} %fusion.49), channel_id=1, source_target_pairs={{0,1},{1,0},{2,3},{3,2},{4,5},{5,4},{6,7},{7,6},{8,9},{9,8},{10,11... | collective-permute-start | bytes 786440 | tf_op jit(solution)/shard_map/ppermute | solution.py:22
  147.7 12.2 %collective-permute-start.29 = (bf16[128,1536]{1,0:T(8,128)(2,1)S(1)}, bf16[128,1536]{1,0:T(8,128)(2,1)S(1)}, u32[]{:S(2)}, u32[]{:S(2)}) collective-permute-start(bf16[128,1536]{1,0:T(8,128)(2,1)S(1)} %add_convert_fusion.2), channel_id=1, source_target_pairs={{0,2},{2,0},{1,3},{3,1},{4,6},{6,4},{5,7},{7,5},{8,10},{10,8},{9,1... | collective-permute-start | bytes 1179656 | tf_op jit(solution)/shard_map/ppermute | solution.py:27
  166.3 4.7 %collective-permute-start.31 = (f32[4,1024]{1,0:T(4,128)S(1)}, f32[4,1024]{1,0:T(4,128)S(1)}, u32[]{:S(2)}, u32[]{:S(2)}) collective-permute-start(f32[4,1024]{1,0:T(4,128)S(1)} %fusion.79), channel_id=1, source_target_pairs={{0,16},{8,24},{16,0},{24,8},{1,17},{9,25},{17,1},{25,9},{2,18},{10... | collective-permute-start | bytes 49160 | tf_op jit(solution)/shard_map/ppermute | solution.py:27
  176.4 6.0 %collective-permute-start.33 = (f32[128,1792]{1,0:T(8,128)S(1)}, f32[128,1792]{1,0:T(8,128)S(1)}, u32[]{:S(2)}, u32[]{:S(2)}) collective-permute-start(f32[128,1792]{1,0:T(8,128)S(1)} %constant_dynamic-slice_fusion.3), channel_id=1, source_target_pairs={{0,2},{2,0},{1,3},{3,1},{4,6},{6,4},{5,7},{7,5},{8,10},{10,8},{9,1... | collective-permute-start | bytes 2752520 | tf_op jit(solution)/shard_map/ppermute | solution.py:27
  186.8 22.3 %collective-permute-start.37 = (bf16[2,128,1792]{2,1,0:T(8,128)(2,1)S(1)}, bf16[2,128,1792]{2,1,0:T(8,128)(2,1)S(1)}, u32[]{:S(2)}, u32[]{:S(2)}) collective-permute-start(bf16[2,128,1792]{2,1,0:T(8,128)(2,1)S(1)} %pad_maximum_fusion.3), channel_id=1, source_target_pairs={{0,1},{1,0},{2,3},{3,2},{4,5},{5,4},{6,7},{7,6},{8,9},{9,8},{10,11... | collective-permute-start | bytes 2752520 | tf_op jit(solution)/shard_map/ppermute | solution.py:22
  (28 other events, 131.4 us)

commit v2 on v1

--- a/solution.py
+++ b/solution.py
@@ -219,14 +219,18 @@
     parts_table = [dot(back_table, weight, ((1,), (1,))) for weight in table_weights[1:]]
     sent_text, parts_table, back_text, loss_total = lax.optimization_barrier((sent_text, parts_table, back_text, loss_total))
     sent_table = [add_cores(part).astype(BF16) for part in parts_table]
-    sent = [jnp.stack(pair) for pair in zip(sent_text, sent_table)]
+    cut = sent_text[0].shape[0] // 4
+    first_grads = swap_parts([part[:cut] for part in sent_text])
+    sent = [jnp.concatenate([first[cut:], second], 0) for first, second in zip(sent_text, sent_table)]
     own_text = dot(back_text, text_weights[0], ((1,), (1,)))
     own_table = dot(back_table, table_weights[0], ((1,), (1,)))
-    own_text, own_table, sent = lax.optimization_barrier((own_text, own_table, sent))
-    grads = swap_parts(sent)
+    own_text, own_table, sent, first_grads = lax.optimization_barrier((own_text, own_table, sent, first_grads))
+    grads = [jnp.concatenate(parts, 0) for parts in zip(first_grads, swap_parts(sent))]
     loss_total = cube_sum(loss_total, "core")
-    grad_text = add_cores(own_text) + sum(part[0].astype(F32) for part in grads)
-    grad_table = add_cores(own_table) + sum(part[1].astype(F32) for part in grads)
+    grad_text, grad_table = add_cores(own_text), add_cores(own_table)
+    for part in grads:
+        got_text, got_table = jnp.split(part, 2)
+        grad_text, grad_table = grad_text + got_text.astype(F32), grad_table + got_table.astype(F32)
     return grad_table, grad_text, loss_total / features
 
 

time: 212 us -> 214 us (level)
    ppermute x7 -> x8, starting transfers between devices: 8.97 us -> 10.3 us  [shift(): return lax.ppermute(x, axis, [(i, (i + step) % size) for i in range(size)])]
    unnamed x28 -> x30, local copies, waits for them, and re-layouts: 10.8 us -> 10.3 us
    ppermute x7 -> x8, waiting for transfers between devices: 39.9 us -> 39.4 us  [shift(): return lax.ppermute(x, axis, [(i, (i + step) % size) for i in range(size)])]
  transfers between devices with their start and end apart: 40 -> 41, of which waited for: 20 -> 21; matrix products, arithmetic and copies ran while one was open for 10% -> 10% of each run, Pallas kernels for 4% -> 4%
where the time goes in v2:
time: 214 us; the launch traced here: 213 us
  waiting for transfers between devices  120 us (56%)
  starting transfers between devices  43.6 us (20%)
  matrix products  15.7 us (7%)
  local copies, waits for them, and re-layouts  12.7 us (6%)
  other arithmetic  8.41 us (4%)
  Pallas kernels  7.73 us (4%)
  between operations  4.67 us (2%)
    ppermute x29, waiting for transfers between devices, flip(): return lax.ppermute(x, axis, [(i, i ^ bit) for i in range(size)])  59.4 us
    ppermute x8, waiting for transfers between devices, shift(): return lax.ppermute(x, axis, [(i, (i + step) % size) for i in range(size)])  39.4 us
    ppermute x29, starting transfers between devices, flip(): return lax.ppermute(x, axis, [(i, i ^ bit) for i in range(size)])  27.2 us
    ppermute x1, waiting for transfers between devices, body(): lax.ppermute(mid, 'z', [(1, 0), (2, 3)])  21.4 us
    dot_general x16, matrix products, dot(): return lax.dot_general(a, b, (dims, ((), ())), preferred_element_type=F32)  15.7 us
    ppermute x8, starting transfers between devices, shift(): return lax.ppermute(x, axis, [(i, (i + step) % size) for i in range(size)])  10.3 us
    unnamed x30, local copies, waits for them, and re-layouts  10.3 us
    pallas_call x1, Pallas kernels, weight_blocks(): pl.pallas_call(cut_kernel, out_shape=[jax.ShapeDtypeStruct((rows, cols),...  7.73 us
  transfers between devices with their start and end apart: 41, of which 21 were waited for; matrix products, arithmetic and copies ran while one was open for 10% of the time, Pallas kernels for 4%

profile of v2, /device:TPU:0, one launch (start us, length us, event | category | flops | bytes accessed | tf_op | source)
XLA Modules:
  0.0 213.1 jit_solution(8378865093094160230)
XLA Ops:
  1.2 2.9 %collective-permute-start.2 = (bf16[128,1792]{1,0:T(8,128)(2,1)}, bf16[128,1792]{1,0:T(8,128)(2,1)S(1)}, u32[]{:S(2)}, u32[]{:S(2)}) collective-permute-start(bf16[128,1792]{1,0:T(8,128)(2,1)} %param.4), channel_id=1, source_target_pairs={{0,1},{1,0},{2,3},{3,2},{4,5},{5,4},{6,7},{7,6},{8,9},{9,8},{10,11... | collective-permute-start | bytes 1376264 | tf_op jit(solution)/shard_map/ppermute | solution.py:22
  4.3 7.7 %shard_map.67 = (bf16[1792,1024]{1,0:T(8,128)(2,1)S(1)}, bf16[1792,1024]{1,0:T(8,128)(2,1)S(1)}, bf16[1792,1024]{1,0:T(8,128)(2,1)S(1)}, bf16[1792,1024]{1,0:T(8,128)(2,1)}) custom-call(s32[3]{0:T(128)S(1)} %pad_add_fusion.starts, bf16[3584,2048]{1,0:T(8,128)(2,1)} %refs_0_.1, bf16[3584,2048]{1,0:T(8,128)(2,1)} %refs_1_.1), custom_call_target="tpu_custom_call" | custom-call | tf_op jit(solution)/shard_map/pallas_call | solution.py:78
  16.0 8.9 %collective-permute-done.3 = bf16[128,1792]{1,0:T(8,128)(2,1)S(1)} collective-permute-done((bf16[128,1792]{1,0:T(8,128)(2,1)}, bf16[128,1792]{1,0:T(8,128)(2,1)S(1)}, u32[]{:S(2)}, u32[]{:S(2)}) %collective-permute-start.3) | collective-permute-done | bytes 458784 | tf_op jit(solution)/shard_map/ppermute | solution.py:22
  32.4 2.1 collective-permute-done.6
  34.5 2.9 %collective-permute-start.7 = (f32[5,1024]{1,0:T(8,128)S(1)}, f32[5,1024]{1,0:T(8,128)S(1)}, u32[]{:S(2)}, u32[]{:S(2)}) collective-permute-start(f32[5,1024]{1,0:T(8,128)S(1)} %pad_maximum_fusion.10), channel_id=1, source_target_pairs={{0,16},{8,24},{16,0},{24,8},{1,17},{9,25},{17,1},{25,9},{2,18},{10... | collective-permute-start | bytes 61448 | tf_op jit(solution)/shard_map/ppermute | solution.py:27
  41.3 2.1 %collective-permute-done.8 = f32[5,1024]{1,0:T(8,128)S(1)} collective-permute-done((f32[5,1024]{1,0:T(8,128)S(1)}, f32[5,1024]{1,0:T(8,128)S(1)}, u32[]{:S(2)}, u32[]{:S(2)}) %collective-permute-start.8) | collective-permute-done | bytes 20512 | tf_op jit(solution)/shard_map/ppermute | solution.py:27
  49.1 3.5 %collective-permute-start.9 = (bf16[2,256,1024]{2,1,0:T(8,128)(2,1)S(1)}, bf16[2,256,1024]{2,1,0:T(8,128)(2,1)}, u32[]{:S(2)}, u32[]{:S(2)}) collective-permute-start(bf16[2,256,1024]{2,1,0:T(8,128)(2,1)S(1)} %pad_maximum_fusion), channel_id=1, source_target_pairs={{0,8},{8,0},{16,24},{24,16},{1,9},{9,1},{17,25},{25,17},{2,10},{10... | collective-permute-start | bytes 3145736 | tf_op jit(solution)/shard_map/ppermute | solution.py:27
  52.6 16.8 %collective-permute-done.11 = bf16[2,256,1024]{2,1,0:T(8,128)(2,1)} collective-permute-done((bf16[2,256,1024]{2,1,0:T(8,128)(2,1)S(1)}, bf16[2,256,1024]{2,1,0:T(8,128)(2,1)}, u32[]{:S(2)}, u32[]{:S(2)}) %collective-permute-start.11) | collective-permute-done | bytes 1048608 | tf_op jit(solution)/shard_map/ppermute | solution.py:27
  69.4 2.7 %collective-permute-done.9 = bf16[2,256,1024]{2,1,0:T(8,128)(2,1)} collective-permute-done((bf16[2,256,1024]{2,1,0:T(8,128)(2,1)S(1)}, bf16[2,256,1024]{2,1,0:T(8,128)(2,1)}, u32[]{:S(2)}, u32[]{:S(2)}) %collective-permute-start.9) | collective-permute-done | bytes 1048608 | tf_op jit(solution)/shard_map/ppermute | solution.py:27
  75.7 21.4 %collective-permute-done.13 = bf16[2,256,1024]{2,1,0:T(8,128)(2,1)} collective-permute-done((bf16[2,256,1024]{2,1,0:T(8,128)(2,1)}, bf16[2,256,1024]{2,1,0:T(8,128)(2,1)}, u32[]{:S(2)}, u32[]{:S(2)}) %collective-permute-start.13) | collective-permute-done | bytes 1048608 | tf_op jit(solution)/shard_map/ppermute | solution.py:174
  100.4 2.1 bitcast_dynamic-update-slice_fusion.7
  103.4 2.1 bitcast_dynamic-update-slice_fusion.6
  105.5 2.1 bitcast_dynamic-update-slice_fusion.5
  107.5 11.5 %collective-permute-done.16 = bf16[2,256,1024]{2,1,0:T(8,128)(2,1)S(1)} collective-permute-done((bf16[2,256,1024]{2,1,0:T(8,128)(2,1)S(1)}, bf16[2,256,1024]{2,1,0:T(8,128)(2,1)S(1)}, u32[]{:S(2)}, u32[]{:S(2)}) %collective-permute-start.16) | collective-permute-done | bytes 1048608 | tf_op jit(solution)/shard_map/ppermute | solution.py:27
  123.8 3.8 %collective-permute-start.19 = (bf16[2,128,1024]{2,1,0:T(8,128)(2,1)S(1)}, bf16[2,128,1024]{2,1,0:T(8,128)(2,1)S(1)}, u32[]{:S(2)}, u32[]{:S(2)}) collective-permute-start(bf16[2,128,1024]{2,1,0:T(8,128)(2,1)S(1)} %slice.161), channel_id=1, source_target_pairs={{0,8},{8,0},{16,24},{24,16},{1,9},{9,1},{17,25},{25,17},{2,10},{10... | collective-permute-start | bytes 1572872 | tf_op jit(solution)/shard_map/ppermute | solution.py:27
  130.1 7.5 %collective-permute-done.18 = bf16[2,128,1024]{2,1,0:T(8,128)(2,1)S(1)} collective-permute-done((bf16[2,128,1024]{2,1,0:T(8,128)(2,1)S(1)}, bf16[2,128,1024]{2,1,0:T(8,128)(2,1)S(1)}, u32[]{:S(2)}, u32[]{:S(2)}) %collective-permute-start.18) | collective-permute-done | bytes 524320 | tf_op jit(solution)/shard_map/ppermute | solution.py:27
  137.6 2.3 %collective-permute-done.19 = bf16[2,128,1024]{2,1,0:T(8,128)(2,1)S(1)} collective-permute-done((bf16[2,128,1024]{2,1,0:T(8,128)(2,1)S(1)}, bf16[2,128,1024]{2,1,0:T(8,128)(2,1)S(1)}, u32[]{:S(2)}, u32[]{:S(2)}) %collective-permute-start.19) | collective-permute-done | bytes 524320 | tf_op jit(solution)/shard_map/ppermute | solution.py:27
  139.9 3.0 %collective-permute-done.22 = bf16[128,768]{1,0:T(8,128)(2,1)S(1)} collective-permute-done((bf16[128,768]{1,0:T(8,128)(2,1)S(1)}, bf16[128,768]{1,0:T(8,128)(2,1)S(1)}, u32[]{:S(2)}, u32[]{:S(2)}) %collective-permute-start.22) | collective-permute-done | bytes 196640 | tf_op jit(solution)/shard_map/ppermute | solution.py:22
  147.8 9.4 %collective-permute-done.27 = bf16[128,1024]{1,0:T(8,128)(2,1)S(1)} collective-permute-done((bf16[128,1024]{1,0:T(8,128)(2,1)S(1)}, bf16[128,1024]{1,0:T(8,128)(2,1)S(1)}, u32[]{:S(2)}, u32[]{:S(2)}) %collective-permute-start.27) | collective-permute-done | bytes 262176 | tf_op jit(solution)/shard_map/ppermute | solution.py:22
  162.8 3.5 %collective-permute-done.30 = f32[4,1024]{1,0:T(4,128)S(1)} collective-permute-done((f32[4,1024]{1,0:T(4,128)S(1)}, f32[4,1024]{1,0:T(4,128)S(1)}, u32[]{:S(2)}, u32[]{:S(2)}) %collective-permute-start.30) | collective-permute-done | bytes 16416 | tf_op jit(solution)/shard_map/ppermute | solution.py:27
  167.6 3.4 %collective-permute-done.31 = f32[4,1024]{1,0:T(4,128)S(1)} collective-permute-done((f32[4,1024]{1,0:T(4,128)S(1)}, f32[4,1024]{1,0:T(4,128)S(1)}, u32[]{:S(2)}, u32[]{:S(2)}) %collective-permute-start.31) | collective-permute-done | bytes 16416 | tf_op jit(solution)/shard_map/ppermute | solution.py:27
  172.6 2.2 %collective-permute-done.32 = f32[4,1024]{1,0:T(4,128)S(1)} collective-permute-done((f32[4,1024]{1,0:T(4,128)S(1)}, f32[4,1024]{1,0:T(4,128)S(1)}, u32[]{:S(2)}, u32[]{:S(2)}) %collective-permute-start.32) | collective-permute-done | bytes 16416 | tf_op jit(solution)/shard_map/ppermute | solution.py:27
  187.7 2.1 collective-permute-done.36
  194.4 16.0 %collective-permute-done.38 = bf16[224,1792]{1,0:T(8,128)(2,1)S(1)} collective-permute-done((bf16[224,1792]{1,0:T(8,128)(2,1)S(1)}, bf16[224,1792]{1,0:T(8,128)(2,1)S(1)}, u32[]{:S(2)}, u32[]{:S(2)}) %collective-permute-start.38) | collective-permute-done | bytes 802848 | tf_op jit(solution)/shard_map/ppermute | solution.py:22
  (168 shorter events, 66.4 us)
Async XLA Ops:
  0.6 11.4 %collective-permute-start.1 = (bf16[128,1792]{1,0:T(8,128)(2,1)}, bf16[128,1792]{1,0:T(8,128)(2,1)S(1)}, u32[]{:S(2)}, u32[]{:S(2)}) collective-permute-start(bf16[128,1792]{1,0:T(8,128)(2,1)} %param.5), channel_id=1, source_target_pairs={{0,2},{2,0},{1,3},{3,1},{4,6},{6,4},{5,7},{7,5},{8,10},{10,8},{9,1... | collective-permute-start | bytes 1376264 | tf_op jit(solution)/shard_map/ppermute | solution.py:27
  1.1 12.6 %collective-permute-start = (bf16[128,1792]{1,0:T(8,128)(2,1)}, bf16[128,1792]{1,0:T(8,128)(2,1)S(1)}, u32[]{:S(2)}, u32[]{:S(2)}) collective-permute-start(bf16[128,1792]{1,0:T(8,128)(2,1)} %param.4), channel_id=1, source_target_pairs={{0,2},{2,0},{1,3},{3,1},{4,6},{6,4},{5,7},{7,5},{8,10},{10,8},{9,1... | collective-permute-start | bytes 1376264 | tf_op jit(solution)/shard_map/ppermute | solution.py:27
  1.2 14.8 %collective-permute-start.2 = (bf16[128,1792]{1,0:T(8,128)(2,1)}, bf16[128,1792]{1,0:T(8,128)(2,1)S(1)}, u32[]{:S(2)}, u32[]{:S(2)}) collective-permute-start(bf16[128,1792]{1,0:T(8,128)(2,1)} %param.4), channel_id=1, source_target_pairs={{0,1},{1,0},{2,3},{3,2},{4,5},{5,4},{6,7},{7,6},{8,9},{9,8},{10,11... | collective-permute-start | bytes 1376264 | tf_op jit(solution)/shard_map/ppermute | solution.py:22
  4.1 20.8 %collective-permute-start.3 = (bf16[128,1792]{1,0:T(8,128)(2,1)}, bf16[128,1792]{1,0:T(8,128)(2,1)S(1)}, u32[]{:S(2)}, u32[]{:S(2)}) collective-permute-start(bf16[128,1792]{1,0:T(8,128)(2,1)} %param.5), channel_id=1, source_target_pairs={{0,1},{1,0},{2,3},{3,2},{4,5},{5,4},{6,7},{7,6},{8,9},{9,8},{10,11... | collective-permute-start | bytes 1376264 | tf_op jit(solution)/shard_map/ppermute | solution.py:22
  45.7 6.9 %collective-permute-start.10 = (bf16[2,256,1024]{2,1,0:T(8,128)(2,1)S(1)}, bf16[2,256,1024]{2,1,0:T(8,128)(2,1)}, u32[]{:S(2)}, u32[]{:S(2)}) collective-permute-start(bf16[2,256,1024]{2,1,0:T(8,128)(2,1)S(1)} %pad_maximum_fusion), channel_id=1, source_target_pairs={{8,16},{16,8},{9,17},{17,9},{10,18},{18,10},{11,19},{19,11},{12,20... | collective-permute-start | bytes 3145736 | tf_op jit(solution)/shard_map/ppermute | solution.py:172
  47.4 22.1 %collective-permute-start.11 = (bf16[2,256,1024]{2,1,0:T(8,128)(2,1)S(1)}, bf16[2,256,1024]{2,1,0:T(8,128)(2,1)}, u32[]{:S(2)}, u32[]{:S(2)}) collective-permute-start(bf16[2,256,1024]{2,1,0:T(8,128)(2,1)S(1)} %pad_maximum_fusion), channel_id=1, source_target_pairs={{0,4},{4,0},{1,5},{5,1},{2,6},{6,2},{3,7},{7,3},{8,12},{12,8},{9,1... | collective-permute-start | bytes 3145736 | tf_op jit(solution)/shard_map/ppermute | solution.py:27
  49.1 23.0 %collective-permute-start.9 = (bf16[2,256,1024]{2,1,0:T(8,128)(2,1)S(1)}, bf16[2,256,1024]{2,1,0:T(8,128)(2,1)}, u32[]{:S(2)}, u32[]{:S(2)}) collective-permute-start(bf16[2,256,1024]{2,1,0:T(8,128)(2,1)S(1)} %pad_maximum_fusion), channel_id=1, source_target_pairs={{0,8},{8,0},{16,24},{24,16},{1,9},{9,1},{17,25},{25,17},{2,10},{10... | collective-permute-start | bytes 3145736 | tf_op jit(solution)/shard_map/ppermute | solution.py:27
  73.8 23.2 %collective-permute-start.13 = (bf16[2,256,1024]{2,1,0:T(8,128)(2,1)}, bf16[2,256,1024]{2,1,0:T(8,128)(2,1)}, u32[]{:S(2)}, u32[]{:S(2)}) collective-permute-start(bf16[2,256,1024]{2,1,0:T(8,128)(2,1)} %collective-permute-done.10), channel_id=1, source_target_pairs={{8,0},{16,24},{9,1},{17,25},{10,2},{18,26},{11,3},{19,27},{12,4},{... | collective-permute-start | bytes 3145736 | tf_op jit(solution)/shard_map/ppermute | solution.py:174
  75.1 22.0 %collective-permute-start.14 = (bf16[2,256,1024]{2,1,0:T(8,128)(2,1)}, bf16[2,256,1024]{2,1,0:T(8,128)(2,1)}, u32[]{:S(2)}, u32[]{:S(2)}) collective-permute-start(bf16[2,256,1024]{2,1,0:T(8,128)(2,1)} %collective-permute-done.9), channel_id=1, source_target_pairs={{0,4},{4,0},{1,5},{5,1},{2,6},{6,2},{3,7},{7,3},{8,12},{12,8},{9,1... | collective-permute-start | bytes 3145736 | tf_op jit(solution)/shard_map/ppermute | solution.py:27
  97.0 22.0 %collective-permute-start.15 = (bf16[2,256,1024]{2,1,0:T(8,128)(2,1)}, bf16[2,256,1024]{2,1,0:T(8,128)(2,1)S(1)}, u32[]{:S(2)}, u32[]{:S(2)}) collective-permute-start(bf16[2,256,1024]{2,1,0:T(8,128)(2,1)} %collective-permute-done.12), channel_id=1, source_target_pairs={{8,0},{16,24},{9,1},{17,25},{10,2},{18,26},{11,3},{19,27},{12,4},{... | collective-permute-start | bytes 3145736 | tf_op jit(solution)/shard_map/ppermute | solution.py:177
  99.9 19.2 %collective-permute-start.16 = (bf16[2,256,1024]{2,1,0:T(8,128)(2,1)S(1)}, bf16[2,256,1024]{2,1,0:T(8,128)(2,1)S(1)}, u32[]{:S(2)}, u32[]{:S(2)}) collective-permute-start(bf16[2,256,1024]{2,1,0:T(8,128)(2,1)S(1)} %broadcast_select_fusion.1), channel_id=1, source_target_pairs={{0,4},{4,0},{1,5},{5,1},{2,6},{6,2},{3,7},{7,3},{8,12},{12,8},{9,1... | collective-permute-start | bytes 3145736 | tf_op jit(solution)/shard_map/ppermute | solution.py:27
  121.1 6.5 %collective-permute-start.20 = (f32[128,1536]{1,0:T(8,128)S(1)}, f32[128,1536]{1,0:T(8,128)S(1)}, u32[]{:S(2)}, u32[]{:S(2)}) collective-permute-start(f32[128,1536]{1,0:T(8,128)S(1)} %constant_dynamic-slice_fusion.6), channel_id=1, source_target_pairs={{0,2},{2,0},{1,3},{3,1},{4,6},{6,4},{5,7},{7,5},{8,10},{10,8},{9,1... | collective-permute-start | bytes 2359304 | tf_op jit(solution)/shard_map/ppermute | solution.py:27
  123.0 6.3 %collective-permute-start.17 = (f32[128,1536]{1,0:T(8,128)S(1)}, f32[128,1536]{1,0:T(8,128)S(1)}, u32[]{:S(2)}, u32[]{:S(2)}) collective-permute-start(f32[128,1536]{1,0:T(8,128)S(1)} %constant_dynamic-slice_fusion.7), channel_id=1, source_target_pairs={{0,2},{2,0},{1,3},{3,1},{4,6},{6,4},{5,7},{7,5},{8,10},{10,8},{9,1... | collective-permute-start | bytes 2359304 | tf_op jit(solution)/shard_map/ppermute | solution.py:27
  123.2 14.4 %collective-permute-start.18 = (bf16[2,128,1024]{2,1,0:T(8,128)(2,1)S(1)}, bf16[2,128,1024]{2,1,0:T(8,128)(2,1)S(1)}, u32[]{:S(2)}, u32[]{:S(2)}) collective-permute-start(bf16[2,128,1024]{2,1,0:T(8,128)(2,1)S(1)} %slice.197), channel_id=1, source_target_pairs={{0,4},{4,0},{1,5},{5,1},{2,6},{6,2},{3,7},{7,3},{8,12},{12,8},{9,1... | collective-permute-start | bytes 1572872 | tf_op jit(solution)/shard_map/ppermute | solution.py:27
  123.8 16.1 %collective-permute-start.19 = (bf16[2,128,1024]{2,1,0:T(8,128)(2,1)S(1)}, bf16[2,128,1024]{2,1,0:T(8,128)(2,1)S(1)}, u32[]{:S(2)}, u32[]{:S(2)}) collective-permute-start(bf16[2,128,1024]{2,1,0:T(8,128)(2,1)S(1)} %slice.161), channel_id=1, source_target_pairs={{0,8},{8,0},{16,24},{24,16},{1,9},{9,1},{17,25},{25,17},{2,10},{10... | collective-permute-start | bytes 1572872 | tf_op jit(solution)/shard_map/ppermute | solution.py:27
  127.7 15.2 %collective-permute-start.21 = (bf16[128,1536]{1,0:T(8,128)(2,1)S(1)}, bf16[128,1536]{1,0:T(8,128)(2,1)S(1)}, u32[]{:S(2)}, u32[]{:S(2)}) collective-permute-start(bf16[128,1536]{1,0:T(8,128)(2,1)S(1)} %fusion.54), channel_id=1, source_target_pairs={{0,1},{1,0},{2,3},{3,2},{4,5},{5,4},{6,7},{7,6},{8,9},{9,8},{10,11... | collective-permute-start | bytes 1179656 | tf_op jit(solution)/shard_map/ppermute | solution.py:22
  129.5 13.5 %collective-permute-start.22 = (bf16[128,768]{1,0:T(8,128)(2,1)S(1)}, bf16[128,768]{1,0:T(8,128)(2,1)S(1)}, u32[]{:S(2)}, u32[]{:S(2)}) collective-permute-start(bf16[128,768]{1,0:T(8,128)(2,1)S(1)} %get-tuple-element.105), channel_id=1, source_target_pairs={{0,1},{1,0},{2,3},{3,2},{4,5},{5,4},{6,7},{7,6},{8,9},{9,8},{10,11... | collective-permute-start | bytes 589832 | tf_op jit(solution)/shard_map/ppermute | solution.py:22
  144.7 12.6 %collective-permute-start.23 = (bf16[128,768]{1,0:T(8,128)(2,1)S(1)}, bf16[128,768]{1,0:T(8,128)(2,1)S(1)}, u32[]{:S(2)}, u32[]{:S(2)}) collective-permute-start(bf16[128,768]{1,0:T(8,128)(2,1)S(1)} %get-tuple-element.104), channel_id=1, source_target_pairs={{0,1},{1,0},{2,3},{3,2},{4,5},{5,4},{6,7},{7,6},{8,9},{9,8},{10,11... | collective-permute-start | bytes 589832 | tf_op jit(solution)/shard_map/ppermute | solution.py:22
  146.4 10.8 %collective-permute-start.27 = (bf16[128,1024]{1,0:T(8,128)(2,1)S(1)}, bf16[128,1024]{1,0:T(8,128)(2,1)S(1)}, u32[]{:S(2)}, u32[]{:S(2)}) collective-permute-start(bf16[128,1024]{1,0:T(8,128)(2,1)S(1)} %fusion.48), channel_id=1, source_target_pairs={{0,1},{1,0},{2,3},{3,2},{4,5},{5,4},{6,7},{7,6},{8,9},{9,8},{10,11... | collective-permute-start | bytes 786440 | tf_op jit(solution)/shard_map/ppermute | solution.py:22
  147.7 12.2 %collective-permute-start.29 = (bf16[128,1536]{1,0:T(8,128)(2,1)S(1)}, bf16[128,1536]{1,0:T(8,128)(2,1)S(1)}, u32[]{:S(2)}, u32[]{:S(2)}) collective-permute-start(bf16[128,1536]{1,0:T(8,128)(2,1)S(1)} %add_convert_fusion.2), channel_id=1, source_target_pairs={{0,2},{2,0},{1,3},{3,1},{4,6},{6,4},{5,7},{7,5},{8,10},{10,8},{9,1... | collective-permute-start | bytes 1179656 | tf_op jit(solution)/shard_map/ppermute | solution.py:27
  176.4 6.0 %collective-permute-start.33 = (f32[128,1792]{1,0:T(8,128)S(1)}, f32[128,1792]{1,0:T(8,128)S(1)}, u32[]{:S(2)}, u32[]{:S(2)}) collective-permute-start(f32[128,1792]{1,0:T(8,128)S(1)} %constant_dynamic-slice_fusion.3), channel_id=1, source_target_pairs={{0,2},{2,0},{1,3},{3,1},{4,6},{6,4},{5,7},{7,5},{8,10},{10,8},{9,1... | collective-permute-start | bytes 2752520 | tf_op jit(solution)/shard_map/ppermute | solution.py:27
  189.8 20.6 %collective-permute-start.37 = (f32[128,1792]{1,0:T(8,128)S(1)}, f32[128,1792]{1,0:T(8,128)S(1)}, u32[]{:S(2)}, u32[]{:S(2)}) collective-permute-start(f32[128,1792]{1,0:T(8,128)S(1)} %constant_dynamic-slice_fusion.1), channel_id=1, source_target_pairs={{0,2},{2,0},{1,3},{3,1},{4,6},{6,4},{5,7},{7,5},{8,10},{10,8},{9,1... | collective-permute-start | bytes 2752520 | tf_op jit(solution)/shard_map/ppermute | solution.py:27
  190.0 20.4 %collective-permute-start.39 = (f32[128,1792]{1,0:T(8,128)S(1)}, f32[128,1792]{1,0:T(8,128)S(1)}, u32[]{:S(2)}, u32[]{:S(2)}) collective-permute-start(f32[128,1792]{1,0:T(8,128)S(1)} %constant_dynamic-slice_fusion), channel_id=1, source_target_pairs={{0,2},{2,0},{1,3},{3,1},{4,6},{6,4},{5,7},{7,5},{8,10},{10,8},{9,1... | collective-permute-start | bytes 2752520 | tf_op jit(solution)/shard_map/ppermute | solution.py:27
  190.5 19.9 %collective-permute-start.38 = (bf16[224,1792]{1,0:T(8,128)(2,1)S(1)}, bf16[224,1792]{1,0:T(8,128)(2,1)S(1)}, u32[]{:S(2)}, u32[]{:S(2)}) collective-permute-start(bf16[224,1792]{1,0:T(8,128)(2,1)S(1)} %pad_maximum_fusion.3), channel_id=1, source_target_pairs={{0,1},{1,0},{2,3},{3,2},{4,5},{5,4},{6,7},{7,6},{8,9},{9,8},{10,11... | collective-permute-start | bytes 2408456 | tf_op jit(solution)/shard_map/ppermute | solution.py:22
  (31 other events, 142.4 us)

commit v3 on v1

--- a/solution.py
+++ b/solution.py
@@ -209,7 +209,7 @@
 
     squares = means[3] - diag_weight * diag
     terms = (1.0 - diag) * (1.0 - diag) - OFF_WEIGHT * diag * diag + squares
-    loss_total = cube_sum(jnp.sum(terms).reshape(1), "feat")
+    loss_part = jnp.sum(terms).reshape(1)
 
     back_text = backward(d_text, normed_text, inverse_text, means[:2])
     parts_text = [dot(back_text, weight, ((1,), (1,))) for weight in text_weights[1:]]
@@ -217,12 +217,13 @@
     sent_text = [add_cores(part).astype(BF16) for part in parts_text]
     back_table = backward(d_table, normed_table, inverse_table, means[2:])
     parts_table = [dot(back_table, weight, ((1,), (1,))) for weight in table_weights[1:]]
-    sent_text, parts_table, back_text, loss_total = lax.optimization_barrier((sent_text, parts_table, back_text, loss_total))
+    sent_text, parts_table, back_text, loss_part = lax.optimization_barrier((sent_text, parts_table, back_text, loss_part))
+    loss_total = cube_sum(loss_part, "feat")
     sent_table = [add_cores(part).astype(BF16) for part in parts_table]
     sent = [jnp.stack(pair) for pair in zip(sent_text, sent_table)]
     own_text = dot(back_text, text_weights[0], ((1,), (1,)))
     own_table = dot(back_table, table_weights[0], ((1,), (1,)))
-    own_text, own_table, sent = lax.optimization_barrier((own_text, own_table, sent))
+    own_text, own_table, sent, loss_total = lax.optimization_barrier((own_text, own_table, sent, loss_total))
     grads = swap_parts(sent)
     loss_total = cube_sum(loss_total, "core")
     grad_text = add_cores(own_text) + sum(part[0].astype(F32) for part in grads)

time: 212 us -> 214 us (level)
  local copies, waits for them, and re-layouts: 12.5 us -> 14.8 us
    unnamed x28, local copies, waits for them, and re-layouts: 10.8 us -> 13.2 us
where the time goes in v3:
time: 214 us
  waiting for transfers between devices  121 us (57%)
  starting transfers between devices  42.3 us (20%)
  matrix products  15.6 us (7%)
  local copies, waits for them, and re-layouts  14.8 us (7%)
  other arithmetic  8.43 us (4%)
  Pallas kernels  7.61 us (4%)
  between operations  4.31 us (2%)
    ppermute x29, waiting for transfers between devices, flip(): return lax.ppermute(x, axis, [(i, i ^ bit) for i in range(size)])  59.7 us
    ppermute x7, waiting for transfers between devices, shift(): return lax.ppermute(x, axis, [(i, (i + step) % size) for i in range(size)])  39.9 us
    ppermute x29, starting transfers between devices, flip(): return lax.ppermute(x, axis, [(i, i ^ bit) for i in range(size)])  26.9 us
    ppermute x1, waiting for transfers between devices, body(): lax.ppermute(mid, 'z', [(1, 0), (2, 3)])  21.4 us
    dot_general x16, matrix products, dot(): return lax.dot_general(a, b, (dims, ((), ())), preferred_element_type=F32)  15.6 us
    unnamed x28, local copies, waits for them, and re-layouts  13.2 us
    ppermute x7, starting transfers between devices, shift(): return lax.ppermute(x, axis, [(i, (i + step) % size) for i in range(size)])  9.29 us
    pallas_call x1, Pallas kernels, weight_blocks(): pl.pallas_call(cut_kernel, out_shape=[jax.ShapeDtypeStruct((rows, cols),...  7.61 us
  transfers between devices with their start and end apart: 40, of which 20 were waited for; matrix products, arithmetic and copies ran while one was open for 10% of the time, Pallas kernels for 4%

profile of v3, /device:TPU:0, one launch (start us, length us, event | category | flops | bytes accessed | tf_op | source)
XLA Modules:
  0.0 214.0 jit_solution(17319648250374148870)
XLA Ops:
  1.2 2.9 %collective-permute-start.2 = (bf16[128,1792]{1,0:T(8,128)(2,1)}, bf16[128,1792]{1,0:T(8,128)(2,1)S(1)}, u32[]{:S(2)}, u32[]{:S(2)}) collective-permute-start(bf16[128,1792]{1,0:T(8,128)(2,1)} %param.4), channel_id=1, source_target_pairs={{0,1},{1,0},{2,3},{3,2},{4,5},{5,4},{6,7},{7,6},{8,9},{9,8},{10,11... | collective-permute-start | bytes 1376264 | tf_op jit(solution)/shard_map/ppermute | solution.py:22
  4.3 7.6 %shard_map.67 = (bf16[1792,1024]{1,0:T(8,128)(2,1)S(1)}, bf16[1792,1024]{1,0:T(8,128)(2,1)S(1)}, bf16[1792,1024]{1,0:T(8,128)(2,1)S(1)}, bf16[1792,1024]{1,0:T(8,128)(2,1)}) custom-call(s32[3]{0:T(128)S(1)} %pad_add_fusion.starts, bf16[3584,2048]{1,0:T(8,128)(2,1)} %refs_0_.1, bf16[3584,2048]{1,0:T(8,128)(2,1)} %refs_1_.1), custom_call_target="tpu_custom_call" | custom-call | tf_op jit(solution)/shard_map/pallas_call | solution.py:78
  16.1 8.9 %collective-permute-done.3 = bf16[128,1792]{1,0:T(8,128)(2,1)S(1)} collective-permute-done((bf16[128,1792]{1,0:T(8,128)(2,1)}, bf16[128,1792]{1,0:T(8,128)(2,1)S(1)}, u32[]{:S(2)}, u32[]{:S(2)}) %collective-permute-start.3) | collective-permute-done | bytes 458784 | tf_op jit(solution)/shard_map/ppermute | solution.py:22
  32.4 2.1 collective-permute-done.6
  34.5 2.9 %collective-permute-start.7 = (f32[5,1024]{1,0:T(8,128)S(1)}, f32[5,1024]{1,0:T(8,128)S(1)}, u32[]{:S(2)}, u32[]{:S(2)}) collective-permute-start(f32[5,1024]{1,0:T(8,128)S(1)} %pad_maximum_fusion.9), channel_id=1, source_target_pairs={{0,16},{8,24},{16,0},{24,8},{1,17},{9,25},{17,1},{25,9},{2,18},{10... | collective-permute-start | bytes 61448 | tf_op jit(solution)/shard_map/ppermute | solution.py:27
  37.4 2.0 collective-permute-done.7
  41.3 2.1 %collective-permute-done.8 = f32[5,1024]{1,0:T(8,128)S(1)} collective-permute-done((f32[5,1024]{1,0:T(8,128)S(1)}, f32[5,1024]{1,0:T(8,128)S(1)}, u32[]{:S(2)}, u32[]{:S(2)}) %collective-permute-start.8) | collective-permute-done | bytes 20512 | tf_op jit(solution)/shard_map/ppermute | solution.py:27
  49.1 3.5 %collective-permute-start.9 = (bf16[2,256,1024]{2,1,0:T(8,128)(2,1)S(1)}, bf16[2,256,1024]{2,1,0:T(8,128)(2,1)}, u32[]{:S(2)}, u32[]{:S(2)}) collective-permute-start(bf16[2,256,1024]{2,1,0:T(8,128)(2,1)S(1)} %pad_maximum_fusion), channel_id=1, source_target_pairs={{0,8},{8,0},{16,24},{24,16},{1,9},{9,1},{17,25},{25,17},{2,10},{10... | collective-permute-start | bytes 3145736 | tf_op jit(solution)/shard_map/ppermute | solution.py:27
  52.6 16.8 %collective-permute-done.11 = bf16[2,256,1024]{2,1,0:T(8,128)(2,1)} collective-permute-done((bf16[2,256,1024]{2,1,0:T(8,128)(2,1)S(1)}, bf16[2,256,1024]{2,1,0:T(8,128)(2,1)}, u32[]{:S(2)}, u32[]{:S(2)}) %collective-permute-start.11) | collective-permute-done | bytes 1048608 | tf_op jit(solution)/shard_map/ppermute | solution.py:27
  69.4 2.8 %collective-permute-done.9 = bf16[2,256,1024]{2,1,0:T(8,128)(2,1)} collective-permute-done((bf16[2,256,1024]{2,1,0:T(8,128)(2,1)S(1)}, bf16[2,256,1024]{2,1,0:T(8,128)(2,1)}, u32[]{:S(2)}, u32[]{:S(2)}) %collective-permute-start.9) | collective-permute-done | bytes 1048608 | tf_op jit(solution)/shard_map/ppermute | solution.py:27
  75.7 21.4 %collective-permute-done.13 = bf16[2,256,1024]{2,1,0:T(8,128)(2,1)} collective-permute-done((bf16[2,256,1024]{2,1,0:T(8,128)(2,1)}, bf16[2,256,1024]{2,1,0:T(8,128)(2,1)}, u32[]{:S(2)}, u32[]{:S(2)}) %collective-permute-start.13) | collective-permute-done | bytes 1048608 | tf_op jit(solution)/shard_map/ppermute | solution.py:174
  100.4 2.1 bitcast_dynamic-update-slice_fusion.7
  103.4 2.1 bitcast_dynamic-update-slice_fusion.6
  105.5 2.1 bitcast_dynamic-update-slice_fusion.5
  107.5 11.5 %collective-permute-done.16 = bf16[2,256,1024]{2,1,0:T(8,128)(2,1)S(1)} collective-permute-done((bf16[2,256,1024]{2,1,0:T(8,128)(2,1)S(1)}, bf16[2,256,1024]{2,1,0:T(8,128)(2,1)S(1)}, u32[]{:S(2)}, u32[]{:S(2)}) %collective-permute-start.16) | collective-permute-done | bytes 1048608 | tf_op jit(solution)/shard_map/ppermute | solution.py:27
  123.8 3.8 %collective-permute-start.19 = (bf16[2,128,1024]{2,1,0:T(8,128)(2,1)S(1)}, bf16[2,128,1024]{2,1,0:T(8,128)(2,1)S(1)}, u32[]{:S(2)}, u32[]{:S(2)}) collective-permute-start(bf16[2,128,1024]{2,1,0:T(8,128)(2,1)S(1)} %slice.161), channel_id=1, source_target_pairs={{0,8},{8,0},{16,24},{24,16},{1,9},{9,1},{17,25},{25,17},{2,10},{10... | collective-permute-start | bytes 1572872 | tf_op jit(solution)/shard_map/ppermute | solution.py:27
  130.1 7.5 %collective-permute-done.18 = bf16[2,128,1024]{2,1,0:T(8,128)(2,1)S(1)} collective-permute-done((bf16[2,128,1024]{2,1,0:T(8,128)(2,1)S(1)}, bf16[2,128,1024]{2,1,0:T(8,128)(2,1)S(1)}, u32[]{:S(2)}, u32[]{:S(2)}) %collective-permute-start.18) | collective-permute-done | bytes 524320 | tf_op jit(solution)/shard_map/ppermute | solution.py:27
  137.6 2.3 %collective-permute-done.19 = bf16[2,128,1024]{2,1,0:T(8,128)(2,1)S(1)} collective-permute-done((bf16[2,128,1024]{2,1,0:T(8,128)(2,1)S(1)}, bf16[2,128,1024]{2,1,0:T(8,128)(2,1)S(1)}, u32[]{:S(2)}, u32[]{:S(2)}) %collective-permute-start.19) | collective-permute-done | bytes 524320 | tf_op jit(solution)/shard_map/ppermute | solution.py:27
  139.9 3.0 %collective-permute-done.22 = bf16[128,768]{1,0:T(8,128)(2,1)S(1)} collective-permute-done((bf16[128,768]{1,0:T(8,128)(2,1)S(1)}, bf16[128,768]{1,0:T(8,128)(2,1)S(1)}, u32[]{:S(2)}, u32[]{:S(2)}) %collective-permute-start.22) | collective-permute-done | bytes 196640 | tf_op jit(solution)/shard_map/ppermute | solution.py:22
  147.8 9.4 %collective-permute-done.27 = bf16[128,1024]{1,0:T(8,128)(2,1)S(1)} collective-permute-done((bf16[128,1024]{1,0:T(8,128)(2,1)S(1)}, bf16[128,1024]{1,0:T(8,128)(2,1)S(1)}, u32[]{:S(2)}, u32[]{:S(2)}) %collective-permute-start.27) | collective-permute-done | bytes 262176 | tf_op jit(solution)/shard_map/ppermute | solution.py:22
  162.8 3.5 %collective-permute-done.30 = f32[4,1024]{1,0:T(4,128)S(1)} collective-permute-done((f32[4,1024]{1,0:T(4,128)S(1)}, f32[4,1024]{1,0:T(4,128)S(1)}, u32[]{:S(2)}, u32[]{:S(2)}) %collective-permute-start.30) | collective-permute-done | bytes 16416 | tf_op jit(solution)/shard_map/ppermute | solution.py:27
  167.6 3.4 %collective-permute-done.31 = f32[4,1024]{1,0:T(4,128)S(1)} collective-permute-done((f32[4,1024]{1,0:T(4,128)S(1)}, f32[4,1024]{1,0:T(4,128)S(1)}, u32[]{:S(2)}, u32[]{:S(2)}) %collective-permute-start.31) | collective-permute-done | bytes 16416 | tf_op jit(solution)/shard_map/ppermute | solution.py:27
  172.6 2.2 %collective-permute-done.32 = f32[4,1024]{1,0:T(4,128)S(1)} collective-permute-done((f32[4,1024]{1,0:T(4,128)S(1)}, f32[4,1024]{1,0:T(4,128)S(1)}, u32[]{:S(2)}, u32[]{:S(2)}) %collective-permute-start.32) | collective-permute-done | bytes 16416 | tf_op jit(solution)/shard_map/ppermute | solution.py:27
  192.8 18.6 %collective-permute-done.37 = bf16[2,128,1792]{2,1,0:T(8,128)(2,1)S(1)} collective-permute-done((bf16[2,128,1792]{2,1,0:T(8,128)(2,1)S(1)}, bf16[2,128,1792]{2,1,0:T(8,128)(2,1)S(1)}, u32[]{:S(2)}, u32[]{:S(2)}) %collective-permute-start.37) | collective-permute-done | bytes 917536 | tf_op jit(solution)/shard_map/ppermute | solution.py:22
  (161 shorter events, 65.4 us)
Async XLA Ops:
  0.6 11.3 %collective-permute-start.1 = (bf16[128,1792]{1,0:T(8,128)(2,1)}, bf16[128,1792]{1,0:T(8,128)(2,1)S(1)}, u32[]{:S(2)}, u32[]{:S(2)}) collective-permute-start(bf16[128,1792]{1,0:T(8,128)(2,1)} %param.5), channel_id=1, source_target_pairs={{0,2},{2,0},{1,3},{3,1},{4,6},{6,4},{5,7},{7,5},{8,10},{10,8},{9,1... | collective-permute-start | bytes 1376264 | tf_op jit(solution)/shard_map/ppermute | solution.py:27
  1.1 12.5 %collective-permute-start = (bf16[128,1792]{1,0:T(8,128)(2,1)}, bf16[128,1792]{1,0:T(8,128)(2,1)S(1)}, u32[]{:S(2)}, u32[]{:S(2)}) collective-permute-start(bf16[128,1792]{1,0:T(8,128)(2,1)} %param.4), channel_id=1, source_target_pairs={{0,2},{2,0},{1,3},{3,1},{4,6},{6,4},{5,7},{7,5},{8,10},{10,8},{9,1... | collective-permute-start | bytes 1376264 | tf_op jit(solution)/shard_map/ppermute | solution.py:27
  1.2 14.8 %collective-permute-start.2 = (bf16[128,1792]{1,0:T(8,128)(2,1)}, bf16[128,1792]{1,0:T(8,128)(2,1)S(1)}, u32[]{:S(2)}, u32[]{:S(2)}) collective-permute-start(bf16[128,1792]{1,0:T(8,128)(2,1)} %param.4), channel_id=1, source_target_pairs={{0,1},{1,0},{2,3},{3,2},{4,5},{5,4},{6,7},{7,6},{8,9},{9,8},{10,11... | collective-permute-start | bytes 1376264 | tf_op jit(solution)/shard_map/ppermute | solution.py:22
  4.1 20.8 %collective-permute-start.3 = (bf16[128,1792]{1,0:T(8,128)(2,1)}, bf16[128,1792]{1,0:T(8,128)(2,1)S(1)}, u32[]{:S(2)}, u32[]{:S(2)}) collective-permute-start(bf16[128,1792]{1,0:T(8,128)(2,1)} %param.5), channel_id=1, source_target_pairs={{0,1},{1,0},{2,3},{3,2},{4,5},{5,4},{6,7},{7,6},{8,9},{9,8},{10,11... | collective-permute-start | bytes 1376264 | tf_op jit(solution)/shard_map/ppermute | solution.py:22
  34.5 4.9 %collective-permute-start.7 = (f32[5,1024]{1,0:T(8,128)S(1)}, f32[5,1024]{1,0:T(8,128)S(1)}, u32[]{:S(2)}, u32[]{:S(2)}) collective-permute-start(f32[5,1024]{1,0:T(8,128)S(1)} %pad_maximum_fusion.9), channel_id=1, source_target_pairs={{0,16},{8,24},{16,0},{24,8},{1,17},{9,25},{17,1},{25,9},{2,18},{10... | collective-permute-start | bytes 61448 | tf_op jit(solution)/shard_map/ppermute | solution.py:27
  45.7 6.9 %collective-permute-start.10 = (bf16[2,256,1024]{2,1,0:T(8,128)(2,1)S(1)}, bf16[2,256,1024]{2,1,0:T(8,128)(2,1)}, u32[]{:S(2)}, u32[]{:S(2)}) collective-permute-start(bf16[2,256,1024]{2,1,0:T(8,128)(2,1)S(1)} %pad_maximum_fusion), channel_id=1, source_target_pairs={{8,16},{16,8},{9,17},{17,9},{10,18},{18,10},{11,19},{19,11},{12,20... | collective-permute-start | bytes 3145736 | tf_op jit(solution)/shard_map/ppermute | solution.py:172
  47.3 22.1 %collective-permute-start.11 = (bf16[2,256,1024]{2,1,0:T(8,128)(2,1)S(1)}, bf16[2,256,1024]{2,1,0:T(8,128)(2,1)}, u32[]{:S(2)}, u32[]{:S(2)}) collective-permute-start(bf16[2,256,1024]{2,1,0:T(8,128)(2,1)S(1)} %pad_maximum_fusion), channel_id=1, source_target_pairs={{0,4},{4,0},{1,5},{5,1},{2,6},{6,2},{3,7},{7,3},{8,12},{12,8},{9,1... | collective-permute-start | bytes 3145736 | tf_op jit(solution)/shard_map/ppermute | solution.py:27
  49.1 23.0 %collective-permute-start.9 = (bf16[2,256,1024]{2,1,0:T(8,128)(2,1)S(1)}, bf16[2,256,1024]{2,1,0:T(8,128)(2,1)}, u32[]{:S(2)}, u32[]{:S(2)}) collective-permute-start(bf16[2,256,1024]{2,1,0:T(8,128)(2,1)S(1)} %pad_maximum_fusion), channel_id=1, source_target_pairs={{0,8},{8,0},{16,24},{24,16},{1,9},{9,1},{17,25},{25,17},{2,10},{10... | collective-permute-start | bytes 3145736 | tf_op jit(solution)/shard_map/ppermute | solution.py:27
  73.8 23.2 %collective-permute-start.13 = (bf16[2,256,1024]{2,1,0:T(8,128)(2,1)}, bf16[2,256,1024]{2,1,0:T(8,128)(2,1)}, u32[]{:S(2)}, u32[]{:S(2)}) collective-permute-start(bf16[2,256,1024]{2,1,0:T(8,128)(2,1)} %collective-permute-done.10), channel_id=1, source_target_pairs={{8,0},{16,24},{9,1},{17,25},{10,2},{18,26},{11,3},{19,27},{12,4},{... | collective-permute-start | bytes 3145736 | tf_op jit(solution)/shard_map/ppermute | solution.py:174
  75.1 22.0 %collective-permute-start.14 = (bf16[2,256,1024]{2,1,0:T(8,128)(2,1)}, bf16[2,256,1024]{2,1,0:T(8,128)(2,1)}, u32[]{:S(2)}, u32[]{:S(2)}) collective-permute-start(bf16[2,256,1024]{2,1,0:T(8,128)(2,1)} %collective-permute-done.9), channel_id=1, source_target_pairs={{0,4},{4,0},{1,5},{5,1},{2,6},{6,2},{3,7},{7,3},{8,12},{12,8},{9,1... | collective-permute-start | bytes 3145736 | tf_op jit(solution)/shard_map/ppermute | solution.py:27
  97.0 22.0 %collective-permute-start.15 = (bf16[2,256,1024]{2,1,0:T(8,128)(2,1)}, bf16[2,256,1024]{2,1,0:T(8,128)(2,1)S(1)}, u32[]{:S(2)}, u32[]{:S(2)}) collective-permute-start(bf16[2,256,1024]{2,1,0:T(8,128)(2,1)} %collective-permute-done.12), channel_id=1, source_target_pairs={{8,0},{16,24},{9,1},{17,25},{10,2},{18,26},{11,3},{19,27},{12,4},{... | collective-permute-start | bytes 3145736 | tf_op jit(solution)/shard_map/ppermute | solution.py:177
  99.8 19.2 %collective-permute-start.16 = (bf16[2,256,1024]{2,1,0:T(8,128)(2,1)S(1)}, bf16[2,256,1024]{2,1,0:T(8,128)(2,1)S(1)}, u32[]{:S(2)}, u32[]{:S(2)}) collective-permute-start(bf16[2,256,1024]{2,1,0:T(8,128)(2,1)S(1)} %broadcast_select_fusion.1), channel_id=1, source_target_pairs={{0,4},{4,0},{1,5},{5,1},{2,6},{6,2},{3,7},{7,3},{8,12},{12,8},{9,1... | collective-permute-start | bytes 3145736 | tf_op jit(solution)/shard_map/ppermute | solution.py:27
  121.1 6.5 %collective-permute-start.20 = (f32[128,1536]{1,0:T(8,128)S(1)}, f32[128,1536]{1,0:T(8,128)S(1)}, u32[]{:S(2)}, u32[]{:S(2)}) collective-permute-start(f32[128,1536]{1,0:T(8,128)S(1)} %constant_dynamic-slice_fusion.6), channel_id=1, source_target_pairs={{0,2},{2,0},{1,3},{3,1},{4,6},{6,4},{5,7},{7,5},{8,10},{10,8},{9,1... | collective-permute-start | bytes 2359304 | tf_op jit(solution)/shard_map/ppermute | solution.py:27
  123.0 6.3 %collective-permute-start.17 = (f32[128,1536]{1,0:T(8,128)S(1)}, f32[128,1536]{1,0:T(8,128)S(1)}, u32[]{:S(2)}, u32[]{:S(2)}) collective-permute-start(f32[128,1536]{1,0:T(8,128)S(1)} %constant_dynamic-slice_fusion.7), channel_id=1, source_target_pairs={{0,2},{2,0},{1,3},{3,1},{4,6},{6,4},{5,7},{7,5},{8,10},{10,8},{9,1... | collective-permute-start | bytes 2359304 | tf_op jit(solution)/shard_map/ppermute | solution.py:27
  123.2 14.4 %collective-permute-start.18 = (bf16[2,128,1024]{2,1,0:T(8,128)(2,1)S(1)}, bf16[2,128,1024]{2,1,0:T(8,128)(2,1)S(1)}, u32[]{:S(2)}, u32[]{:S(2)}) collective-permute-start(bf16[2,128,1024]{2,1,0:T(8,128)(2,1)S(1)} %slice.197), channel_id=1, source_target_pairs={{0,4},{4,0},{1,5},{5,1},{2,6},{6,2},{3,7},{7,3},{8,12},{12,8},{9,1... | collective-permute-start | bytes 1572872 | tf_op jit(solution)/shard_map/ppermute | solution.py:27
  123.8 16.1 %collective-permute-start.19 = (bf16[2,128,1024]{2,1,0:T(8,128)(2,1)S(1)}, bf16[2,128,1024]{2,1,0:T(8,128)(2,1)S(1)}, u32[]{:S(2)}, u32[]{:S(2)}) collective-permute-start(bf16[2,128,1024]{2,1,0:T(8,128)(2,1)S(1)} %slice.161), channel_id=1, source_target_pairs={{0,8},{8,0},{16,24},{24,16},{1,9},{9,1},{17,25},{25,17},{2,10},{10... | collective-permute-start | bytes 1572872 | tf_op jit(solution)/shard_map/ppermute | solution.py:27
  127.7 15.2 %collective-permute-start.21 = (bf16[128,1536]{1,0:T(8,128)(2,1)S(1)}, bf16[128,1536]{1,0:T(8,128)(2,1)S(1)}, u32[]{:S(2)}, u32[]{:S(2)}) collective-permute-start(bf16[128,1536]{1,0:T(8,128)(2,1)S(1)} %fusion.55), channel_id=1, source_target_pairs={{0,1},{1,0},{2,3},{3,2},{4,5},{5,4},{6,7},{7,6},{8,9},{9,8},{10,11... | collective-permute-start | bytes 1179656 | tf_op jit(solution)/shard_map/ppermute | solution.py:22
  129.5 13.5 %collective-permute-start.22 = (bf16[128,768]{1,0:T(8,128)(2,1)S(1)}, bf16[128,768]{1,0:T(8,128)(2,1)S(1)}, u32[]{:S(2)}, u32[]{:S(2)}) collective-permute-start(bf16[128,768]{1,0:T(8,128)(2,1)S(1)} %get-tuple-element.105), channel_id=1, source_target_pairs={{0,1},{1,0},{2,3},{3,2},{4,5},{5,4},{6,7},{7,6},{8,9},{9,8},{10,11... | collective-permute-start | bytes 589832 | tf_op jit(solution)/shard_map/ppermute | solution.py:22
  144.7 12.6 %collective-permute-start.23 = (bf16[128,768]{1,0:T(8,128)(2,1)S(1)}, bf16[128,768]{1,0:T(8,128)(2,1)S(1)}, u32[]{:S(2)}, u32[]{:S(2)}) collective-permute-start(bf16[128,768]{1,0:T(8,128)(2,1)S(1)} %get-tuple-element.104), channel_id=1, source_target_pairs={{0,1},{1,0},{2,3},{3,2},{4,5},{5,4},{6,7},{7,6},{8,9},{9,8},{10,11... | collective-permute-start | bytes 589832 | tf_op jit(solution)/shard_map/ppermute | solution.py:22
  146.4 10.8 %collective-permute-start.27 = (bf16[128,1024]{1,0:T(8,128)(2,1)S(1)}, bf16[128,1024]{1,0:T(8,128)(2,1)S(1)}, u32[]{:S(2)}, u32[]{:S(2)}) collective-permute-start(bf16[128,1024]{1,0:T(8,128)(2,1)S(1)} %fusion.49), channel_id=1, source_target_pairs={{0,1},{1,0},{2,3},{3,2},{4,5},{5,4},{6,7},{7,6},{8,9},{9,8},{10,11... | collective-permute-start | bytes 786440 | tf_op jit(solution)/shard_map/ppermute | solution.py:22
  147.7 12.2 %collective-permute-start.29 = (bf16[128,1536]{1,0:T(8,128)(2,1)S(1)}, bf16[128,1536]{1,0:T(8,128)(2,1)S(1)}, u32[]{:S(2)}, u32[]{:S(2)}) collective-permute-start(bf16[128,1536]{1,0:T(8,128)(2,1)S(1)} %add_convert_fusion.2), channel_id=1, source_target_pairs={{0,2},{2,0},{1,3},{3,1},{4,6},{6,4},{5,7},{7,5},{8,10},{10,8},{9,1... | collective-permute-start | bytes 1179656 | tf_op jit(solution)/shard_map/ppermute | solution.py:27
  166.3 4.7 %collective-permute-start.31 = (f32[4,1024]{1,0:T(4,128)S(1)}, f32[4,1024]{1,0:T(4,128)S(1)}, u32[]{:S(2)}, u32[]{:S(2)}) collective-permute-start(f32[4,1024]{1,0:T(4,128)S(1)} %fusion.79), channel_id=1, source_target_pairs={{0,16},{8,24},{16,0},{24,8},{1,17},{9,25},{17,1},{25,9},{2,18},{10... | collective-permute-start | bytes 49160 | tf_op jit(solution)/shard_map/ppermute | solution.py:27
  179.7 8.3 %collective-permute-start.34 = (f32[128,1792]{1,0:T(8,128)S(1)}, f32[128,1792]{1,0:T(8,128)S(1)}, u32[]{:S(2)}, u32[]{:S(2)}) collective-permute-start(f32[128,1792]{1,0:T(8,128)S(1)} %constant_dynamic-slice_fusion.2), channel_id=1, source_target_pairs={{0,2},{2,0},{1,3},{3,1},{4,6},{6,4},{5,7},{7,5},{8,10},{10,8},{9,1... | collective-permute-start | bytes 2752520 | tf_op jit(solution)/shard_map/ppermute | solution.py:27
  189.0 22.3 %collective-permute-start.37 = (bf16[2,128,1792]{2,1,0:T(8,128)(2,1)S(1)}, bf16[2,128,1792]{2,1,0:T(8,128)(2,1)S(1)}, u32[]{:S(2)}, u32[]{:S(2)}) collective-permute-start(bf16[2,128,1792]{2,1,0:T(8,128)(2,1)S(1)} %pad_maximum_fusion.3), channel_id=1, source_target_pairs={{0,1},{1,0},{2,3},{3,2},{4,5},{5,4},{6,7},{7,6},{8,9},{9,8},{10,11... | collective-permute-start | bytes 2752520 | tf_op jit(solution)/shard_map/ppermute | solution.py:22
  (28 other events, 133.3 us)

commit v4 on v1

--- a/solution.py
+++ b/solution.py
@@ -166,9 +166,10 @@
     diag_weight = (diag - 1.0).astype(BF16).astype(F32) - OFF_WEIGHT * diag
     normed_table = (z_table - centers[0]) * inverse_table
     normed_text = (z_text - centers[1]) * inverse_text
-    half_table, half_text = normed_table.astype(BF16), normed_text.astype(BF16)
-
-    half = jnp.stack([half_table, half_text])
+    half = jnp.stack([z_table, z_text])
+    half = ((half - centers[:, None]) * lax.rsqrt(spreads[:2] + EPS)[:, None]).astype(BF16)
+    half_table, half_text = half[0], half[1]
+
     near, mid, y_own = lax.optimization_barrier((flip(half, "z"), lax.ppermute(half, "z", [(1, 2), (2, 1)]), over_y(half)))
     far_in, far_end, y_near = lax.optimization_barrier(
         (lax.ppermute(near, "z", [(1, 2), (2, 1)]), lax.ppermute(mid, "z", [(1, 0), (2, 3)]), over_y(near))

time: 212 us -> 210 us (level)
  local copies, waits for them, and re-layouts: 12.5 us -> 6.74 us
  waiting for transfers between devices: 121 us -> 124 us
    unnamed x28 -> x29, local copies, waits for them, and re-layouts: 10.8 us -> 5.92 us
    ppermute x29, waiting for transfers between devices: 59.3 us -> 63 us  [flip(): return lax.ppermute(x, axis, [(i, i ^ bit) for i in range(size)])]
  transfers between devices with their start and end apart: 40 -> 40, of which waited for: 20 -> 20; matrix products, arithmetic and copies ran while one was open for 10% -> 8% of each run, Pallas kernels for 4% -> 4%
where the time goes in v4:
time: 210 us; the launch traced here: 209 us
  waiting for transfers between devices  124 us (59%)
  starting transfers between devices  43.8 us (21%)
  matrix products  15.8 us (8%)
  Pallas kernels  7.73 us (4%)
  local copies, waits for them, and re-layouts  6.74 us (3%)
  other arithmetic  6.44 us (3%)
  between operations  4.58 us (2%)
    ppermute x29, waiting for transfers between devices, flip(): return lax.ppermute(x, axis, [(i, i ^ bit) for i in range(size)])  63 us
    ppermute x7, waiting for transfers between devices, shift(): return lax.ppermute(x, axis, [(i, (i + step) % size) for i in range(size)])  39.9 us
    ppermute x29, starting transfers between devices, flip(): return lax.ppermute(x, axis, [(i, i ^ bit) for i in range(size)])  28.7 us
    ppermute x1, waiting for transfers between devices, body(): lax.ppermute(mid, 'z', [(1, 0), (2, 3)])  21.2 us
    dot_general x16, matrix products, dot(): return lax.dot_general(a, b, (dims, ((), ())), preferred_element_type=F32)  15.8 us
    ppermute x7, starting transfers between devices, shift(): return lax.ppermute(x, axis, [(i, (i + step) % size) for i in range(size)])  8.97 us
    pallas_call x1, Pallas kernels, weight_blocks(): pl.pallas_call(cut_kernel, out_shape=[jax.ShapeDtypeStruct((rows, cols),...  7.73 us
    unnamed x29, local copies, waits for them, and re-layouts  5.92 us
  transfers between devices with their start and end apart: 40, of which 20 were waited for; matrix products, arithmetic and copies ran while one was open for 8% of the time, Pallas kernels for 4%

profile of v4, /device:TPU:0, one launch (start us, length us, event | category | flops | bytes accessed | tf_op | source)
XLA Modules:
  0.0 209.1 jit_solution(3421483979774347606)
XLA Ops:
  1.2 2.9 %collective-permute-start.2 = (bf16[128,1792]{1,0:T(8,128)(2,1)}, bf16[128,1792]{1,0:T(8,128)(2,1)S(1)}, u32[]{:S(2)}, u32[]{:S(2)}) collective-permute-start(bf16[128,1792]{1,0:T(8,128)(2,1)} %param.4), channel_id=1, source_target_pairs={{0,1},{1,0},{2,3},{3,2},{4,5},{5,4},{6,7},{7,6},{8,9},{9,8},{10,11... | collective-permute-start | bytes 1376264 | tf_op jit(solution)/shard_map/ppermute | solution.py:22
  4.3 7.7 %shard_map.67 = (bf16[1792,1024]{1,0:T(8,128)(2,1)S(1)}, bf16[1792,1024]{1,0:T(8,128)(2,1)S(1)}, bf16[1792,1024]{1,0:T(8,128)(2,1)S(1)}, bf16[1792,1024]{1,0:T(8,128)(2,1)}) custom-call(s32[3]{0:T(128)S(1)} %pad_add_fusion.starts, bf16[3584,2048]{1,0:T(8,128)(2,1)} %refs_0_.1, bf16[3584,2048]{1,0:T(8,128)(2,1)} %refs_1_.1), custom_call_target="tpu_custom_call" | custom-call | tf_op jit(solution)/shard_map/pallas_call | solution.py:78
  16.1 8.9 %collective-permute-done.3 = bf16[128,1792]{1,0:T(8,128)(2,1)S(1)} collective-permute-done((bf16[128,1792]{1,0:T(8,128)(2,1)}, bf16[128,1792]{1,0:T(8,128)(2,1)S(1)}, u32[]{:S(2)}, u32[]{:S(2)}) %collective-permute-start.3) | collective-permute-done | bytes 458784 | tf_op jit(solution)/shard_map/ppermute | solution.py:22
  30.5 1.9 collective-permute-start.6
  32.4 2.1 collective-permute-done.6
  34.6 2.9 %collective-permute-start.7 = (f32[5,1024]{1,0:T(8,128)S(1)}, f32[5,1024]{1,0:T(8,128)S(1)}, u32[]{:S(2)}, u32[]{:S(2)}) collective-permute-start(f32[5,1024]{1,0:T(8,128)S(1)} %pad_maximum_fusion.8), channel_id=1, source_target_pairs={{0,16},{8,24},{16,0},{24,8},{1,17},{9,25},{17,1},{25,9},{2,18},{10... | collective-permute-start | bytes 61448 | tf_op jit(solution)/shard_map/ppermute | solution.py:27
  37.5 2.0 collective-permute-done.7
  39.5 1.8 collective-permute-start.8
  41.4 2.1 %collective-permute-done.8 = f32[5,1024]{1,0:T(8,128)S(1)} collective-permute-done((f32[5,1024]{1,0:T(8,128)S(1)}, f32[5,1024]{1,0:T(8,128)S(1)}, u32[]{:S(2)}, u32[]{:S(2)}) %collective-permute-start.8) | collective-permute-done | bytes 20512 | tf_op jit(solution)/shard_map/ppermute | solution.py:27
  47.3 3.5 %collective-permute-start.9 = (bf16[2,256,1024]{2,1,0:T(8,128)(2,1)S(1)}, bf16[2,256,1024]{2,1,0:T(8,128)(2,1)}, u32[]{:S(2)}, u32[]{:S(2)}) collective-permute-start(bf16[2,256,1024]{2,1,0:T(8,128)(2,1)S(1)} %fusion.1), channel_id=1, source_target_pairs={{0,8},{8,0},{16,24},{24,16},{1,9},{9,1},{17,25},{25,17},{2,10},{10... | collective-permute-start | bytes 3145736 | tf_op jit(solution)/shard_map/ppermute | solution.py:27
  50.8 16.7 %collective-permute-done.11 = bf16[2,256,1024]{2,1,0:T(8,128)(2,1)S(1)} collective-permute-done((bf16[2,256,1024]{2,1,0:T(8,128)(2,1)S(1)}, bf16[2,256,1024]{2,1,0:T(8,128)(2,1)S(1)}, u32[]{:S(2)}, u32[]{:S(2)}) %collective-permute-start.11) | collective-permute-done | bytes 1048608 | tf_op jit(solution)/shard_map/ppermute | solution.py:27
  67.5 2.8 %collective-permute-done.9 = bf16[2,256,1024]{2,1,0:T(8,128)(2,1)} collective-permute-done((bf16[2,256,1024]{2,1,0:T(8,128)(2,1)S(1)}, bf16[2,256,1024]{2,1,0:T(8,128)(2,1)}, u32[]{:S(2)}, u32[]{:S(2)}) %collective-permute-start.9) | collective-permute-done | bytes 1048608 | tf_op jit(solution)/shard_map/ppermute | solution.py:27
  74.0 21.2 %collective-permute-done.13 = bf16[2,256,1024]{2,1,0:T(8,128)(2,1)} collective-permute-done((bf16[2,256,1024]{2,1,0:T(8,128)(2,1)}, bf16[2,256,1024]{2,1,0:T(8,128)(2,1)}, u32[]{:S(2)}, u32[]{:S(2)}) %collective-permute-start.13) | collective-permute-done | bytes 1048608 | tf_op jit(solution)/shard_map/ppermute | solution.py:175
  101.9 15.3 %collective-permute-done.16 = bf16[2,256,1024]{2,1,0:T(8,128)(2,1)S(1)} collective-permute-done((bf16[2,256,1024]{2,1,0:T(8,128)(2,1)S(1)}, bf16[2,256,1024]{2,1,0:T(8,128)(2,1)S(1)}, u32[]{:S(2)}, u32[]{:S(2)}) %collective-permute-start.16) | collective-permute-done | bytes 1048608 | tf_op jit(solution)/shard_map/ppermute | solution.py:27
  121.7 3.8 %collective-permute-start.19 = (bf16[2,128,1024]{2,1,0:T(8,128)(2,1)S(1)}, bf16[2,128,1024]{2,1,0:T(8,128)(2,1)S(1)}, u32[]{:S(2)}, u32[]{:S(2)}) collective-permute-start(bf16[2,128,1024]{2,1,0:T(8,128)(2,1)S(1)} %slice.170), channel_id=1, source_target_pairs={{0,8},{8,0},{16,24},{24,16},{1,9},{9,1},{17,25},{25,17},{2,10},{10... | collective-permute-start | bytes 1572872 | tf_op jit(solution)/shard_map/ppermute | solution.py:27
  128.0 6.3 %collective-permute-done.18 = bf16[2,128,1024]{2,1,0:T(8,128)(2,1)S(1)} collective-permute-done((bf16[2,128,1024]{2,1,0:T(8,128)(2,1)S(1)}, bf16[2,128,1024]{2,1,0:T(8,128)(2,1)S(1)}, u32[]{:S(2)}, u32[]{:S(2)}) %collective-permute-start.18) | collective-permute-done | bytes 524320 | tf_op jit(solution)/shard_map/ppermute | solution.py:27
  134.3 3.0 %collective-permute-done.19 = bf16[2,128,1024]{2,1,0:T(8,128)(2,1)S(1)} collective-permute-done((bf16[2,128,1024]{2,1,0:T(8,128)(2,1)S(1)}, bf16[2,128,1024]{2,1,0:T(8,128)(2,1)S(1)}, u32[]{:S(2)}, u32[]{:S(2)}) %collective-permute-start.19) | collective-permute-done | bytes 524320 | tf_op jit(solution)/shard_map/ppermute | solution.py:27
  137.3 3.0 %collective-permute-done.22 = bf16[128,768]{1,0:T(8,128)(2,1)S(1)} collective-permute-done((bf16[128,768]{1,0:T(8,128)(2,1)S(1)}, bf16[128,768]{1,0:T(8,128)(2,1)S(1)}, u32[]{:S(2)}, u32[]{:S(2)}) %collective-permute-start.22) | collective-permute-done | bytes 196640 | tf_op jit(solution)/shard_map/ppermute | solution.py:22
  145.2 9.4 %collective-permute-done.27 = bf16[128,1024]{1,0:T(8,128)(2,1)S(1)} collective-permute-done((bf16[128,1024]{1,0:T(8,128)(2,1)S(1)}, bf16[128,1024]{1,0:T(8,128)(2,1)S(1)}, u32[]{:S(2)}, u32[]{:S(2)}) %collective-permute-start.27) | collective-permute-done | bytes 262176 | tf_op jit(solution)/shard_map/ppermute | solution.py:22
  160.2 3.5 %collective-permute-done.30 = f32[4,1024]{1,0:T(4,128)S(1)} collective-permute-done((f32[4,1024]{1,0:T(4,128)S(1)}, f32[4,1024]{1,0:T(4,128)S(1)}, u32[]{:S(2)}, u32[]{:S(2)}) %collective-permute-start.30) | collective-permute-done | bytes 16416 | tf_op jit(solution)/shard_map/ppermute | solution.py:27
  163.7 1.9 collective-permute-start.31
  165.6 2.8 %collective-permute-done.31 = f32[4,1024]{1,0:T(4,128)S(1)} collective-permute-done((f32[4,1024]{1,0:T(4,128)S(1)}, f32[4,1024]{1,0:T(4,128)S(1)}, u32[]{:S(2)}, u32[]{:S(2)}) %collective-permute-start.31) | collective-permute-done | bytes 16416 | tf_op jit(solution)/shard_map/ppermute | solution.py:27
  169.3 3.0 %collective-permute-done.32 = f32[4,1024]{1,0:T(4,128)S(1)} collective-permute-done((f32[4,1024]{1,0:T(4,128)S(1)}, f32[4,1024]{1,0:T(4,128)S(1)}, u32[]{:S(2)}, u32[]{:S(2)}) %collective-permute-start.32) | collective-permute-done | bytes 16416 | tf_op jit(solution)/shard_map/ppermute | solution.py:27
  188.0 18.5 %collective-permute-done.37 = bf16[2,128,1792]{2,1,0:T(8,128)(2,1)S(1)} collective-permute-done((bf16[2,128,1792]{2,1,0:T(8,128)(2,1)S(1)}, bf16[2,128,1792]{2,1,0:T(8,128)(2,1)S(1)}, u32[]{:S(2)}, u32[]{:S(2)}) %collective-permute-start.37) | collective-permute-done | bytes 917536 | tf_op jit(solution)/shard_map/ppermute | solution.py:22
  (161 shorter events, 57.3 us)
Async XLA Ops:
  0.6 11.4 %collective-permute-start.1 = (bf16[128,1792]{1,0:T(8,128)(2,1)}, bf16[128,1792]{1,0:T(8,128)(2,1)S(1)}, u32[]{:S(2)}, u32[]{:S(2)}) collective-permute-start(bf16[128,1792]{1,0:T(8,128)(2,1)} %param.5), channel_id=1, source_target_pairs={{0,2},{2,0},{1,3},{3,1},{4,6},{6,4},{5,7},{7,5},{8,10},{10,8},{9,1... | collective-permute-start | bytes 1376264 | tf_op jit(solution)/shard_map/ppermute | solution.py:27
  1.1 12.6 %collective-permute-start = (bf16[128,1792]{1,0:T(8,128)(2,1)}, bf16[128,1792]{1,0:T(8,128)(2,1)S(1)}, u32[]{:S(2)}, u32[]{:S(2)}) collective-permute-start(bf16[128,1792]{1,0:T(8,128)(2,1)} %param.4), channel_id=1, source_target_pairs={{0,2},{2,0},{1,3},{3,1},{4,6},{6,4},{5,7},{7,5},{8,10},{10,8},{9,1... | collective-permute-start | bytes 1376264 | tf_op jit(solution)/shard_map/ppermute | solution.py:27
  1.2 14.8 %collective-permute-start.2 = (bf16[128,1792]{1,0:T(8,128)(2,1)}, bf16[128,1792]{1,0:T(8,128)(2,1)S(1)}, u32[]{:S(2)}, u32[]{:S(2)}) collective-permute-start(bf16[128,1792]{1,0:T(8,128)(2,1)} %param.4), channel_id=1, source_target_pairs={{0,1},{1,0},{2,3},{3,2},{4,5},{5,4},{6,7},{7,6},{8,9},{9,8},{10,11... | collective-permute-start | bytes 1376264 | tf_op jit(solution)/shard_map/ppermute | solution.py:22
  4.1 20.8 %collective-permute-start.3 = (bf16[128,1792]{1,0:T(8,128)(2,1)}, bf16[128,1792]{1,0:T(8,128)(2,1)S(1)}, u32[]{:S(2)}, u32[]{:S(2)}) collective-permute-start(bf16[128,1792]{1,0:T(8,128)(2,1)} %param.5), channel_id=1, source_target_pairs={{0,1},{1,0},{2,3},{3,2},{4,5},{5,4},{6,7},{7,6},{8,9},{9,8},{10,11... | collective-permute-start | bytes 1376264 | tf_op jit(solution)/shard_map/ppermute | solution.py:22
  34.6 4.9 %collective-permute-start.7 = (f32[5,1024]{1,0:T(8,128)S(1)}, f32[5,1024]{1,0:T(8,128)S(1)}, u32[]{:S(2)}, u32[]{:S(2)}) collective-permute-start(f32[5,1024]{1,0:T(8,128)S(1)} %pad_maximum_fusion.8), channel_id=1, source_target_pairs={{0,16},{8,24},{16,0},{24,8},{1,17},{9,25},{17,1},{25,9},{2,18},{10... | collective-permute-start | bytes 61448 | tf_op jit(solution)/shard_map/ppermute | solution.py:27
  43.9 6.9 %collective-permute-start.10 = (bf16[2,256,1024]{2,1,0:T(8,128)(2,1)S(1)}, bf16[2,256,1024]{2,1,0:T(8,128)(2,1)}, u32[]{:S(2)}, u32[]{:S(2)}) collective-permute-start(bf16[2,256,1024]{2,1,0:T(8,128)(2,1)S(1)} %fusion.1), channel_id=1, source_target_pairs={{8,16},{16,8},{9,17},{17,9},{10,18},{18,10},{11,19},{19,11},{12,20... | collective-permute-start | bytes 3145736 | tf_op jit(solution)/shard_map/ppermute | solution.py:173
  45.5 22.0 %collective-permute-start.11 = (bf16[2,256,1024]{2,1,0:T(8,128)(2,1)S(1)}, bf16[2,256,1024]{2,1,0:T(8,128)(2,1)S(1)}, u32[]{:S(2)}, u32[]{:S(2)}) collective-permute-start(bf16[2,256,1024]{2,1,0:T(8,128)(2,1)S(1)} %fusion.1), channel_id=1, source_target_pairs={{0,4},{4,0},{1,5},{5,1},{2,6},{6,2},{3,7},{7,3},{8,12},{12,8},{9,1... | collective-permute-start | bytes 3145736 | tf_op jit(solution)/shard_map/ppermute | solution.py:27
  47.3 23.0 %collective-permute-start.9 = (bf16[2,256,1024]{2,1,0:T(8,128)(2,1)S(1)}, bf16[2,256,1024]{2,1,0:T(8,128)(2,1)}, u32[]{:S(2)}, u32[]{:S(2)}) collective-permute-start(bf16[2,256,1024]{2,1,0:T(8,128)(2,1)S(1)} %fusion.1), channel_id=1, source_target_pairs={{0,8},{8,0},{16,24},{24,16},{1,9},{9,1},{17,25},{25,17},{2,10},{10... | collective-permute-start | bytes 3145736 | tf_op jit(solution)/shard_map/ppermute | solution.py:27
  72.0 23.2 %collective-permute-start.13 = (bf16[2,256,1024]{2,1,0:T(8,128)(2,1)}, bf16[2,256,1024]{2,1,0:T(8,128)(2,1)}, u32[]{:S(2)}, u32[]{:S(2)}) collective-permute-start(bf16[2,256,1024]{2,1,0:T(8,128)(2,1)} %collective-permute-done.10), channel_id=1, source_target_pairs={{8,0},{16,24},{9,1},{17,25},{10,2},{18,26},{11,3},{19,27},{12,4},{... | collective-permute-start | bytes 3145736 | tf_op jit(solution)/shard_map/ppermute | solution.py:175
  73.3 21.9 %collective-permute-start.14 = (bf16[2,256,1024]{2,1,0:T(8,128)(2,1)}, bf16[2,256,1024]{2,1,0:T(8,128)(2,1)}, u32[]{:S(2)}, u32[]{:S(2)}) collective-permute-start(bf16[2,256,1024]{2,1,0:T(8,128)(2,1)} %collective-permute-done.9), channel_id=1, source_target_pairs={{0,4},{4,0},{1,5},{5,1},{2,6},{6,2},{3,7},{7,3},{8,12},{12,8},{9,1... | collective-permute-start | bytes 3145736 | tf_op jit(solution)/shard_map/ppermute | solution.py:27
  95.2 22.1 %collective-permute-start.15 = (bf16[2,256,1024]{2,1,0:T(8,128)(2,1)}, bf16[2,256,1024]{2,1,0:T(8,128)(2,1)S(1)}, u32[]{:S(2)}, u32[]{:S(2)}) collective-permute-start(bf16[2,256,1024]{2,1,0:T(8,128)(2,1)} %collective-permute-done.12), channel_id=1, source_target_pairs={{8,0},{16,24},{9,1},{17,25},{10,2},{18,26},{11,3},{19,27},{12,4},{... | collective-permute-start | bytes 3145736 | tf_op jit(solution)/shard_map/ppermute | solution.py:178
  98.0 19.2 %collective-permute-start.16 = (bf16[2,256,1024]{2,1,0:T(8,128)(2,1)S(1)}, bf16[2,256,1024]{2,1,0:T(8,128)(2,1)S(1)}, u32[]{:S(2)}, u32[]{:S(2)}) collective-permute-start(bf16[2,256,1024]{2,1,0:T(8,128)(2,1)S(1)} %broadcast_select_fusion.1), channel_id=1, source_target_pairs={{0,4},{4,0},{1,5},{5,1},{2,6},{6,2},{3,7},{7,3},{8,12},{12,8},{9,1... | collective-permute-start | bytes 3145736 | tf_op jit(solution)/shard_map/ppermute | solution.py:27
  118.5 7.0 %collective-permute-start.20 = (f32[128,1536]{1,0:T(8,128)S(1)}, f32[128,1536]{1,0:T(8,128)S(1)}, u32[]{:S(2)}, u32[]{:S(2)}) collective-permute-start(f32[128,1536]{1,0:T(8,128)S(1)} %constant_dynamic-slice_fusion.6), channel_id=1, source_target_pairs={{0,2},{2,0},{1,3},{3,1},{4,6},{6,4},{5,7},{7,5},{8,10},{10,8},{9,1... | collective-permute-start | bytes 2359304 | tf_op jit(solution)/shard_map/ppermute | solution.py:27
  119.7 7.5 %collective-permute-start.17 = (f32[128,1536]{1,0:T(8,128)S(1)}, f32[128,1536]{1,0:T(8,128)S(1)}, u32[]{:S(2)}, u32[]{:S(2)}) collective-permute-start(f32[128,1536]{1,0:T(8,128)S(1)} %constant_dynamic-slice_fusion.7), channel_id=1, source_target_pairs={{0,2},{2,0},{1,3},{3,1},{4,6},{6,4},{5,7},{7,5},{8,10},{10,8},{9,1... | collective-permute-start | bytes 2359304 | tf_op jit(solution)/shard_map/ppermute | solution.py:27
  120.4 13.9 %collective-permute-start.18 = (bf16[2,128,1024]{2,1,0:T(8,128)(2,1)S(1)}, bf16[2,128,1024]{2,1,0:T(8,128)(2,1)S(1)}, u32[]{:S(2)}, u32[]{:S(2)}) collective-permute-start(bf16[2,128,1024]{2,1,0:T(8,128)(2,1)S(1)} %slice.209), channel_id=1, source_target_pairs={{0,4},{4,0},{1,5},{5,1},{2,6},{6,2},{3,7},{7,3},{8,12},{12,8},{9,1... | collective-permute-start | bytes 1572872 | tf_op jit(solution)/shard_map/ppermute | solution.py:27
  121.7 15.6 %collective-permute-start.19 = (bf16[2,128,1024]{2,1,0:T(8,128)(2,1)S(1)}, bf16[2,128,1024]{2,1,0:T(8,128)(2,1)S(1)}, u32[]{:S(2)}, u32[]{:S(2)}) collective-permute-start(bf16[2,128,1024]{2,1,0:T(8,128)(2,1)S(1)} %slice.170), channel_id=1, source_target_pairs={{0,8},{8,0},{16,24},{24,16},{1,9},{9,1},{17,25},{25,17},{2,10},{10... | collective-permute-start | bytes 1572872 | tf_op jit(solution)/shard_map/ppermute | solution.py:27
  125.6 14.8 %collective-permute-start.21 = (bf16[128,1536]{1,0:T(8,128)(2,1)S(1)}, bf16[128,1536]{1,0:T(8,128)(2,1)S(1)}, u32[]{:S(2)}, u32[]{:S(2)}) collective-permute-start(bf16[128,1536]{1,0:T(8,128)(2,1)S(1)} %fusion.59), channel_id=1, source_target_pairs={{0,1},{1,0},{2,3},{3,2},{4,5},{5,4},{6,7},{7,6},{8,9},{9,8},{10,11... | collective-permute-start | bytes 1179656 | tf_op jit(solution)/shard_map/ppermute | solution.py:22
  127.3 13.1 %collective-permute-start.22 = (bf16[128,768]{1,0:T(8,128)(2,1)S(1)}, bf16[128,768]{1,0:T(8,128)(2,1)S(1)}, u32[]{:S(2)}, u32[]{:S(2)}) collective-permute-start(bf16[128,768]{1,0:T(8,128)(2,1)S(1)} %get-tuple-element.101), channel_id=1, source_target_pairs={{0,1},{1,0},{2,3},{3,2},{4,5},{5,4},{6,7},{7,6},{8,9},{9,8},{10,11... | collective-permute-start | bytes 589832 | tf_op jit(solution)/shard_map/ppermute | solution.py:22
  142.1 12.7 %collective-permute-start.23 = (bf16[128,768]{1,0:T(8,128)(2,1)S(1)}, bf16[128,768]{1,0:T(8,128)(2,1)S(1)}, u32[]{:S(2)}, u32[]{:S(2)}) collective-permute-start(bf16[128,768]{1,0:T(8,128)(2,1)S(1)} %get-tuple-element.100), channel_id=1, source_target_pairs={{0,1},{1,0},{2,3},{3,2},{4,5},{5,4},{6,7},{7,6},{8,9},{9,8},{10,11... | collective-permute-start | bytes 589832 | tf_op jit(solution)/shard_map/ppermute | solution.py:22
  143.8 10.8 %collective-permute-start.27 = (bf16[128,1024]{1,0:T(8,128)(2,1)S(1)}, bf16[128,1024]{1,0:T(8,128)(2,1)S(1)}, u32[]{:S(2)}, u32[]{:S(2)}) collective-permute-start(bf16[128,1024]{1,0:T(8,128)(2,1)S(1)} %fusion.49), channel_id=1, source_target_pairs={{0,1},{1,0},{2,3},{3,2},{4,5},{5,4},{6,7},{7,6},{8,9},{9,8},{10,11... | collective-permute-start | bytes 786440 | tf_op jit(solution)/shard_map/ppermute | solution.py:22
  145.1 12.3 %collective-permute-start.29 = (bf16[128,1536]{1,0:T(8,128)(2,1)S(1)}, bf16[128,1536]{1,0:T(8,128)(2,1)S(1)}, u32[]{:S(2)}, u32[]{:S(2)}) collective-permute-start(bf16[128,1536]{1,0:T(8,128)(2,1)S(1)} %add_convert_fusion.2), channel_id=1, source_target_pairs={{0,2},{2,0},{1,3},{3,1},{4,6},{6,4},{5,7},{7,5},{8,10},{10,8},{9,1... | collective-permute-start | bytes 1179656 | tf_op jit(solution)/shard_map/ppermute | solution.py:27
  163.7 4.7 %collective-permute-start.31 = (f32[4,1024]{1,0:T(4,128)S(1)}, f32[4,1024]{1,0:T(4,128)S(1)}, u32[]{:S(2)}, u32[]{:S(2)}) collective-permute-start(f32[4,1024]{1,0:T(4,128)S(1)} %fusion.84), channel_id=1, source_target_pairs={{0,16},{8,24},{16,0},{24,8},{1,17},{9,25},{17,1},{25,9},{2,18},{10... | collective-permute-start | bytes 49160 | tf_op jit(solution)/shard_map/ppermute | solution.py:27
  173.8 6.0 %collective-permute-start.33 = (f32[128,1792]{1,0:T(8,128)S(1)}, f32[128,1792]{1,0:T(8,128)S(1)}, u32[]{:S(2)}, u32[]{:S(2)}) collective-permute-start(f32[128,1792]{1,0:T(8,128)S(1)} %constant_dynamic-slice_fusion.3), channel_id=1, source_target_pairs={{0,2},{2,0},{1,3},{3,1},{4,6},{6,4},{5,7},{7,5},{8,10},{10,8},{9,1... | collective-permute-start | bytes 2752520 | tf_op jit(solution)/shard_map/ppermute | solution.py:27
  184.2 22.3 %collective-permute-start.37 = (bf16[2,128,1792]{2,1,0:T(8,128)(2,1)S(1)}, bf16[2,128,1792]{2,1,0:T(8,128)(2,1)S(1)}, u32[]{:S(2)}, u32[]{:S(2)}) collective-permute-start(bf16[2,128,1792]{2,1,0:T(8,128)(2,1)S(1)} %pad_maximum_fusion.2), channel_id=1, source_target_pairs={{0,1},{1,0},{2,3},{3,2},{4,5},{5,4},{6,7},{7,6},{8,9},{9,8},{10,11... | collective-permute-start | bytes 2752520 | tf_op jit(solution)/shard_map/ppermute | solution.py:22
  (28 other events, 109.7 us)
